TPU v7x, 32 devices: a whole 2x2x4 slice. The times are simulated.
32 devices in a mesh: blk: 8 (over y, x, core), grp: 4 (over z).
Axes of the slice: x: 2, y: 2, z: 4, core: 2. Of those that a mesh axis runs over, the one named last changes fastest.
Arguments:
- spectra: bfloat16 [2, 64, 4, 4096], P(None, 'blk', None, 'grp'), may hold values from -6 to 6
- quality: int32 [64, 4], P('blk'), may hold values from 0 to 3
- pair_mask: int32 [8, 6, 2, 2], P('blk'), may hold values 0 or 1
- owners: int32 [3072, 1], P('blk'), may hold values from 0 to 7; in each aligned block of 384 rows (0 to 383, 384 to 767, ...) at most 96 rows name the same one
- local_rows: int32 [3072], P('blk'), may hold values from 0 to 15
Outputs:
- stack: float32 [128, 2048], P('blk', 'grp')
Inputs may be any that keep to these rules, and one draw needn't show every extreme that they name: `owners`: among the rows of one block no owner is named more than 96 times, a bound that some block reaches.
All inputs are finite; a program needn't handle non-finite values. No bound on the sum of `pair_mask` on one device may be relied on, other than what follows from the above.
Results may differ from a plain program's by a relative error of at most 0.0033.
Values may be sent and summed in bfloat16 or wider, within the bound.
No kernel may reach another device: no remote copies, remote signals or barrier semaphores. Data moves between devices by JAX's collectives and lax.ppermute only.
A program may use at most 128 MiB of HBM per device.

v0:
```python
import math

import jax
import jax.numpy as jnp
from jax import lax
from jax.sharding import PartitionSpec as P

STA = 8
BINS = 4096
LAGS = 2048
STEPS = 6
SUB = 4
VS_DEV = 16


def from_behind(array, axis, by):
    size = lax.axis_size(axis)
    return lax.ppermute(array, axis, [(i, (i + by) % size) for i in range(size)])


def lag_table(bins_index, total_bins, lags):
    shifts = jnp.arange(lags, dtype=jnp.int32) - lags // 2
    phase = jnp.mod(bins_index[:, None] * shifts[None, :], 2 * total_bins)
    angle = phase.astype(jnp.float32) * (math.pi / total_bins)
    factor = 1.0 / math.sqrt(total_bins)
    return jnp.concatenate([jnp.cos(angle) * factor, -jnp.sin(angle) * factor], axis=0).astype(
        jnp.bfloat16
    )


def phase_rows(own_spec, own_weight, far_spec, far_weight, sub_mask):
    near_weight = own_weight.astype(jnp.float32)[:, :, None]
    away_weight = far_weight.astype(jnp.float32)[:, :, None]
    a_real = own_spec[0].astype(jnp.float32) * near_weight
    a_imag = own_spec[1].astype(jnp.float32) * near_weight
    b_real = far_spec[0].astype(jnp.float32) * away_weight
    b_imag = far_spec[1].astype(jnp.float32) * away_weight
    cross_real = jnp.sum(a_real[:, None] * b_real[None] + a_imag[:, None] * b_imag[None], axis=2)
    cross_imag = jnp.sum(a_imag[:, None] * b_real[None] - a_real[:, None] * b_imag[None], axis=2)
    station_mask = jnp.repeat(jnp.repeat(sub_mask, SUB, axis=0), SUB, axis=1).astype(jnp.float32)
    factor = station_mask[:, :, None] * lax.rsqrt(
        jnp.maximum(cross_real * cross_real + cross_imag * cross_imag, 1.0)
    )
    joined = jnp.concatenate([cross_real * factor, cross_imag * factor], axis=2).astype(
        jnp.bfloat16
    )
    return joined.reshape(STA * STA, joined.shape[2])


def on_device(spectra, quality, pair_mask, owners, local_rows):
    bins_dev = spectra.shape[3]
    blocks = lax.axis_size("blk")
    rows_dev = owners.shape[0]
    capacity = max(2, 2 * rows_dev // blocks)
    masks = pair_mask[0]
    pieces = [None] * STEPS
    visiting = (spectra, quality)
    for offset in range(STEPS):
        visiting = from_behind((visiting[0], visiting[1]), "blk", 1)
        pieces[offset] = phase_rows(spectra, quality, visiting[0], visiting[1], masks[offset])
    rows_all = jnp.concatenate(pieces, axis=0)
    owner_flat = owners[:, 0]
    row_index = jnp.arange(rows_dev, dtype=jnp.int32)
    earlier = (owner_flat[:, None] == owner_flat[None, :]) & (
        row_index[None, :] < row_index[:, None]
    )
    position = jnp.sum(earlier.astype(jnp.int32), axis=1)
    slot_index = owner_flat * capacity + position
    sources = jnp.arange(VS_DEV, dtype=jnp.int32)
    bins_index = lax.axis_index("grp") * bins_dev + jnp.arange(bins_dev, dtype=jnp.int32)
    table = lag_table(bins_index, BINS, LAGS)
    lag_dev = LAGS // lax.axis_size("grp")
    lag_terms = lax.psum_scatter(
        lax.dot_general(
            table, rows_all, (((0,), (1,)), ((), ())), preferred_element_type=jnp.float32
        ),
        "grp",
        scatter_dimension=0,
        tiled=True,
    )
    outgoing = jnp.zeros((lag_dev, blocks * capacity), jnp.float32).at[:, slot_index].set(lag_terms)
    labels = jnp.full((1, blocks * capacity), -1, jnp.int32).at[0, slot_index].set(local_rows)
    received, got_labels = (
        lax.all_to_all(outgoing, "blk", split_axis=1, concat_axis=1, tiled=True),
        lax.all_to_all(labels, "blk", split_axis=1, concat_axis=1, tiled=True),
    )
    selector = (got_labels == sources[:, None]).astype(jnp.float32)
    stack = lax.dot_general(
        selector,
        received,
        (((1,), (1,)), ((), ())),
        precision=lax.Precision.HIGHEST,
        preferred_element_type=jnp.float32,
    )
    return stack


def solution(mesh):
    in_specs = (
        P(None, "blk", None, "grp"),
        P("blk", None),
        P("blk", None, None, None),
        P("blk", None),
        P("blk"),
    )
    out_specs = P("blk", "grp")
    return jax.shard_map(
        on_device, mesh=mesh, in_specs=in_specs, out_specs=out_specs, check_vma=False
    )
```

profile of v0, /device:TPU:0, one launch (start us, length us, event | category | flops | bytes accessed | tf_op | source)
XLA Modules:
  0.0 204.5 jit_solution(1010262168625591818)
XLA Ops:
  7.0 2.6 %collective-permute-start.1 = (s32[8,4]{0,1:T(4,128)}, s32[8,4]{0,1:T(4,128)S(1)}, u32[]{:S(2)}, u32[]{:S(2)}) collective-permute-start(s32[8,4]{0,1:T(4,128)} %param.6), channel_id=1, source_target_pairs={{0,4},{4,8},{8,12},{12,16},{16,20},{20,24},{24,28},{28,0},{1,5},{5... | collective-permute-start | bytes 392 | tf_op jit(solution)/shard_map/ppermute | solution.py:18
  10.4 1.0 slice_convert_fusion
  12.9 35.8 %multiply_convert_fusion.1 = (bf16[1024,2048]{1,0:T(8,128)(2,1)}, bf16[1024,2048]{1,0:T(8,128)(2,1)}) fusion(s32[2048]{0:T(1024)S(1)} %iota_add_fusion, s32[1024]{0:T(1024)S(1)} %iota_add_fusion.1), kind=kLoop, calls=%fused_computation.15 | loop fusion | flops 39845888 | bytes 8400896 | tf_op jit(solution)/shard_map/convert.14
  49.2 3.8 %collective-permute-done.3 = s32[8,4]{0,1:T(4,128)S(1)} collective-permute-done((s32[8,4]{0,1:T(4,128)S(1)}, s32[8,4]{0,1:T(4,128)S(1)}, u32[]{:S(2)}, u32[]{:S(2)}) %collective-permute-start.3) | collective-permute-done | bytes 160 | tf_op jit(solution)/shard_map/ppermute | solution.py:18
  53.0 3.8 %collective-permute-done.5 = s32[8,4]{0,1:T(4,128)S(1)} collective-permute-done((s32[8,4]{0,1:T(4,128)S(1)}, s32[8,4]{0,1:T(4,128)S(1)}, u32[]{:S(2)}, u32[]{:S(2)}) %collective-permute-start.5) | collective-permute-done | bytes 160 | tf_op jit(solution)/shard_map/ppermute | solution.py:18
  56.9 3.8 %collective-permute-done.7 = s32[8,4]{0,1:T(4,128)S(1)} collective-permute-done((s32[8,4]{0,1:T(4,128)S(1)}, s32[8,4]{0,1:T(4,128)S(1)}, u32[]{:S(2)}, u32[]{:S(2)}) %collective-permute-start.7) | collective-permute-done | bytes 160 | tf_op jit(solution)/shard_map/ppermute | solution.py:18
  60.8 3.8 %collective-permute-done.9 = s32[8,4]{0,1:T(4,128)S(1)} collective-permute-done((s32[8,4]{0,1:T(4,128)S(1)}, s32[8,4]{0,1:T(4,128)S(1)}, u32[]{:S(2)}, u32[]{:S(2)}) %collective-permute-start.9) | collective-permute-done | bytes 160 | tf_op jit(solution)/shard_map/ppermute | solution.py:18
  64.8 3.8 %collective-permute-done.11 = s32[8,4]{0,1:T(4,128)S(1)} collective-permute-done((s32[8,4]{0,1:T(4,128)S(1)}, s32[8,4]{0,1:T(4,128)S(1)}, u32[]{:S(2)}, u32[]{:S(2)}) %collective-permute-start.11) | collective-permute-done | bytes 160 | tf_op jit(solution)/shard_map/ppermute | solution.py:18
  68.9 5.0 %collective-permute-done.2 = bf16[2,8,4,1024]{3,2,1,0:T(4,128)(2,1)S(1)} collective-permute-done((bf16[2,8,4,1024]{3,2,1,0:T(4,128)(2,1)S(1)}, bf16[2,8,4,1024]{3,2,1,0:T(4,128)(2,1)S(1)}, u32[]{:S(2)}, u32[]{:S(2)}) %collective-permute-start.2) | collective-permute-done | bytes 131104 | tf_op jit(solution)/shard_map/ppermute | solution.py:18
  74.2 5.0 %collective-permute-done.4 = bf16[2,8,4,1024]{3,2,1,0:T(4,128)(2,1)S(1)} collective-permute-done((bf16[2,8,4,1024]{3,2,1,0:T(4,128)(2,1)S(1)}, bf16[2,8,4,1024]{3,2,1,0:T(4,128)(2,1)S(1)}, u32[]{:S(2)}, u32[]{:S(2)}) %collective-permute-start.4) | collective-permute-done | bytes 131104 | tf_op jit(solution)/shard_map/ppermute | solution.py:18
  79.5 5.0 %collective-permute-done.6 = bf16[2,8,4,1024]{3,2,1,0:T(4,128)(2,1)S(1)} collective-permute-done((bf16[2,8,4,1024]{3,2,1,0:T(4,128)(2,1)S(1)}, bf16[2,8,4,1024]{3,2,1,0:T(4,128)(2,1)S(1)}, u32[]{:S(2)}, u32[]{:S(2)}) %collective-permute-start.6) | collective-permute-done | bytes 131104 | tf_op jit(solution)/shard_map/ppermute | solution.py:18
  84.8 5.0 %collective-permute-done.8 = bf16[2,8,4,1024]{3,2,1,0:T(4,128)(2,1)S(1)} collective-permute-done((bf16[2,8,4,1024]{3,2,1,0:T(4,128)(2,1)S(1)}, bf16[2,8,4,1024]{3,2,1,0:T(4,128)(2,1)S(1)}, u32[]{:S(2)}, u32[]{:S(2)}) %collective-permute-start.8) | collective-permute-done | bytes 131104 | tf_op jit(solution)/shard_map/ppermute | solution.py:18
  90.1 5.0 %collective-permute-done.10 = bf16[2,8,4,1024]{3,2,1,0:T(4,128)(2,1)S(1)} collective-permute-done((bf16[2,8,4,1024]{3,2,1,0:T(4,128)(2,1)S(1)}, bf16[2,8,4,1024]{3,2,1,0:T(4,128)(2,1)S(1)}, u32[]{:S(2)}, u32[]{:S(2)}) %collective-permute-start.10) | collective-permute-done | bytes 131104 | tf_op jit(solution)/shard_map/ppermute | solution.py:18
  95.4 2.7 %add_reduce_fusion = (f32[8,8,1024]{2,1,0:T(8,128)S(1)}, f32[8,8,1024]{2,1,0:T(8,128)S(1)}, f32[8,8,1024]{2,1,0:T(8,128)S(1)}, f32[8,8,1024]{2,1,0:T(8,128)S(1)}...) fusion(f32[8,4,1024]{2,0,1:T(8,128)S(1)} %copy.94, ...), kind=kLoop, calls=%fused_computation.17 | loop fusion | flops 11796480 | bytes 4980736 | tf_op jit(solution)/shard_map/reduce_sum | solution.py:38
  98.8 1.5 copy-done
  100.3 6.2 %fusion.3 = f32[2048,384]{1,0:T(8,128)} fusion(bf16[384,2048]{1,0:T(8,128)(2,1)S(1)} %maximum_dynamic-update-slice_fusion, bf16[1024,2048]{1,0:T(8,128)(2,1)S(1)} %copy-done.1, bf16[1024,2048]{1,0:T(8,128)(2,1)S(1)} %copy-done), kind=kOutput, calls=%fused_computation.10 | convolution fusion | flops 3238002688 | bytes 13107200 | tf_op jit(solution)/shard_map/dot_general | solution.py:74
  106.9 3.1 %scatter_custom_fusion = s32[768]{0:T(1024)S(1)} fusion(s32[384]{0:T(512)S(1)} %fusion.50, s32[384]{0:T(512)} %param.9, s32[]{:T(128)} %constant.13.clone.1), kind=kCustom, calls=%fused_computation.119 | custom fusion | bytes 3584 | tf_op jit(solution)/shard_map/scatter | solution.py:82
  110.6 3.3 %all-to-all-start = ((s32[1,8,96]{2,0,1:T(1,128)}), s32[1,8,96]{2,0,1:T(1,128)S(1)}, u32[]{:S(2)}, u32[]{:S(2)}) async-start(s32[1,8,96]{2,0,1:T(1,128)} %all_to_all.14), calls=%async_computation | async-start | bytes 8192 | tf_op jit(solution)/shard_map/all_to_all | solution.py:85
  114.0 53.4 %reduce-scatter.2.cloned.1.call-done = f32[512,384]{1,0:T(8,128)} async-done(((f32[2048,384]{1,0:T(8,128)}), f32[512,384]{1,0:T(8,128)}) %reduce-scatter.2.cloned.1.call-update) | async-done | bytes 786448 | tf_op jit(solution)/shard_map/reduce_scatter | solution.py:73
  167.3 1.4 copy.97
  168.7 3.0 %scatter_custom_fusion.1 = f32[512,768]{0,1:T(8,128)} fusion(s32[384]{0:T(512)S(1)} %fusion.50, f32[384,512]{1,0:T(8,128)S(1)} %copy.97, f32[]{:T(128)} %constant.17.clone.1), kind=kCustom, calls=%fused_computation.28 | custom fusion | bytes 1572868 | tf_op jit(solution)/shard_map/scatter | solution.py:81
  171.8 3.6 %all-to-all-start.1 = ((f32[512,8,96]{0,2,1:T(8,128)}), f32[512,8,96]{0,2,1:T(8,128)S(1)}, u32[]{:S(2)}, u32[]{:S(2)}) async-start(f32[512,8,96]{0,2,1:T(8,128)} %bitcast.39), calls=%async_computation.2 | async-start | bytes 3145728 | tf_op jit(solution)/shard_map/all_to_all | solution.py:84
  176.7 19.8 %all-to-all-done.1 = f32[512,8,96]{0,2,1:T(8,128)S(1)} async-done(((f32[512,8,96]{0,2,1:T(8,128)}), f32[512,8,96]{0,2,1:T(8,128)S(1)}, u32[]{:S(2)}, u32[]{:S(2)}) %all-to-all-start.1) | async-done | bytes 1572896 | tf_op jit(solution)/shard_map/all_to_all | solution.py:84
  196.4 1.2 fusion.46
  (98 shorter events, 8.1 us)
Async XLA Ops:
  6.5 160.8 %reduce-scatter.2.cloned.1.call-start = ((), (), s32[]{:S(2)}) async-start(), calls=%async_computation.3 | async-start | bytes 3932160 | tf_op jit(solution)/shard_map/reduce_scatter | solution.py:73
  6.5 62.1 %collective-permute-start = (bf16[2,8,4,1024]{3,2,1,0:T(4,128)(2,1)}, bf16[2,8,4,1024]{3,2,1,0:T(4,128)(2,1)S(1)}, u32[]{:S(2)}, u32[]{:S(2)}) collective-permute-start(bf16[2,8,4,1024]{3,2,1,0:T(4,128)(2,1)} %param.5), channel_id=1, source_target_pairs={{0,4},{4,8},{8,12},{12,16},{16,20},{20,24},{24,28},{28,0},{1,5},{5... | collective-permute-start | bytes 393224 | tf_op jit(solution)/shard_map/ppermute | solution.py:18
  7.0 42.0 %collective-permute-start.1 = (s32[8,4]{0,1:T(4,128)}, s32[8,4]{0,1:T(4,128)S(1)}, u32[]{:S(2)}, u32[]{:S(2)}) collective-permute-start(s32[8,4]{0,1:T(4,128)} %param.6), channel_id=1, source_target_pairs={{0,4},{4,8},{8,12},{12,16},{16,20},{20,24},{24,28},{28,0},{1,5},{5... | collective-permute-start | bytes 392 | tf_op jit(solution)/shard_map/ppermute | solution.py:18
  12.9 35.8 %copy-start.2 = (bf16[2,8,4,1024]{3,2,1,0:T(4,128)(2,1)S(1)}, bf16[2,8,4,1024]{3,2,1,0:T(4,128)(2,1)}, u32[]{:S(2)}) copy-start(bf16[2,8,4,1024]{3,2,1,0:T(4,128)(2,1)} %param.5) | copy-start | bytes 393220
  49.0 4.0 %collective-permute-start.3 = (s32[8,4]{0,1:T(4,128)S(1)}, s32[8,4]{0,1:T(4,128)S(1)}, u32[]{:S(2)}, u32[]{:S(2)}) collective-permute-start(s32[8,4]{0,1:T(4,128)S(1)} %collective-permute-done.1), channel_id=1, source_target_pairs={{0,4},{4,8},{8,12},{12,16},{16,20},{20,24},{24,28},{28,0},{1,5},{5... | collective-permute-start | bytes 392 | tf_op jit(solution)/shard_map/ppermute | solution.py:18
  52.9 3.9 %collective-permute-start.5 = (s32[8,4]{0,1:T(4,128)S(1)}, s32[8,4]{0,1:T(4,128)S(1)}, u32[]{:S(2)}, u32[]{:S(2)}) collective-permute-start(s32[8,4]{0,1:T(4,128)S(1)} %collective-permute-done.3), channel_id=1, source_target_pairs={{0,4},{4,8},{8,12},{12,16},{16,20},{20,24},{24,28},{28,0},{1,5},{5... | collective-permute-start | bytes 392 | tf_op jit(solution)/shard_map/ppermute | solution.py:18
  56.8 3.9 %collective-permute-start.7 = (s32[8,4]{0,1:T(4,128)S(1)}, s32[8,4]{0,1:T(4,128)S(1)}, u32[]{:S(2)}, u32[]{:S(2)}) collective-permute-start(s32[8,4]{0,1:T(4,128)S(1)} %collective-permute-done.5), channel_id=1, source_target_pairs={{0,4},{4,8},{8,12},{12,16},{16,20},{20,24},{24,28},{28,0},{1,5},{5... | collective-permute-start | bytes 392 | tf_op jit(solution)/shard_map/ppermute | solution.py:18
  60.8 3.9 %collective-permute-start.9 = (s32[8,4]{0,1:T(4,128)S(1)}, s32[8,4]{0,1:T(4,128)S(1)}, u32[]{:S(2)}, u32[]{:S(2)}) collective-permute-start(s32[8,4]{0,1:T(4,128)S(1)} %collective-permute-done.7), channel_id=1, source_target_pairs={{0,4},{4,8},{8,12},{12,16},{16,20},{20,24},{24,28},{28,0},{1,5},{5... | collective-permute-start | bytes 392 | tf_op jit(solution)/shard_map/ppermute | solution.py:18
  64.7 3.9 %collective-permute-start.11 = (s32[8,4]{0,1:T(4,128)S(1)}, s32[8,4]{0,1:T(4,128)S(1)}, u32[]{:S(2)}, u32[]{:S(2)}) collective-permute-start(s32[8,4]{0,1:T(4,128)S(1)} %collective-permute-done.9), channel_id=1, source_target_pairs={{0,4},{4,8},{8,12},{12,16},{16,20},{20,24},{24,28},{28,0},{1,5},{5... | collective-permute-start | bytes 392 | tf_op jit(solution)/shard_map/ppermute | solution.py:18
  68.7 5.3 %collective-permute-start.2 = (bf16[2,8,4,1024]{3,2,1,0:T(4,128)(2,1)S(1)}, bf16[2,8,4,1024]{3,2,1,0:T(4,128)(2,1)S(1)}, u32[]{:S(2)}, u32[]{:S(2)}) collective-permute-start(bf16[2,8,4,1024]{3,2,1,0:T(4,128)(2,1)S(1)} %collective-permute-done), channel_id=1, source_target_pairs={{0,4},{4,8},{8,12},{12,16},{16,20},{20,24},{24,28},{28,0},{1,5},{5... | collective-permute-start | bytes 393224 | tf_op jit(solution)/shard_map/ppermute | solution.py:18
  74.0 5.3 %collective-permute-start.4 = (bf16[2,8,4,1024]{3,2,1,0:T(4,128)(2,1)S(1)}, bf16[2,8,4,1024]{3,2,1,0:T(4,128)(2,1)S(1)}, u32[]{:S(2)}, u32[]{:S(2)}) collective-permute-start(bf16[2,8,4,1024]{3,2,1,0:T(4,128)(2,1)S(1)} %collective-permute-done.2), channel_id=1, source_target_pairs={{0,4},{4,8},{8,12},{12,16},{16,20},{20,24},{24,28},{28,0},{1,5},{5... | collective-permute-start | bytes 393224 | tf_op jit(solution)/shard_map/ppermute | solution.py:18
  79.2 5.3 %collective-permute-start.6 = (bf16[2,8,4,1024]{3,2,1,0:T(4,128)(2,1)S(1)}, bf16[2,8,4,1024]{3,2,1,0:T(4,128)(2,1)S(1)}, u32[]{:S(2)}, u32[]{:S(2)}) collective-permute-start(bf16[2,8,4,1024]{3,2,1,0:T(4,128)(2,1)S(1)} %collective-permute-done.4), channel_id=1, source_target_pairs={{0,4},{4,8},{8,12},{12,16},{16,20},{20,24},{24,28},{28,0},{1,5},{5... | collective-permute-start | bytes 393224 | tf_op jit(solution)/shard_map/ppermute | solution.py:18
  84.5 5.3 %collective-permute-start.8 = (bf16[2,8,4,1024]{3,2,1,0:T(4,128)(2,1)S(1)}, bf16[2,8,4,1024]{3,2,1,0:T(4,128)(2,1)S(1)}, u32[]{:S(2)}, u32[]{:S(2)}) collective-permute-start(bf16[2,8,4,1024]{3,2,1,0:T(4,128)(2,1)S(1)} %collective-permute-done.6), channel_id=1, source_target_pairs={{0,4},{4,8},{8,12},{12,16},{16,20},{20,24},{24,28},{28,0},{1,5},{5... | collective-permute-start | bytes 393224 | tf_op jit(solution)/shard_map/ppermute | solution.py:18
  89.8 5.3 %collective-permute-start.10 = (bf16[2,8,4,1024]{3,2,1,0:T(4,128)(2,1)S(1)}, bf16[2,8,4,1024]{3,2,1,0:T(4,128)(2,1)S(1)}, u32[]{:S(2)}, u32[]{:S(2)}) collective-permute-start(bf16[2,8,4,1024]{3,2,1,0:T(4,128)(2,1)S(1)} %collective-permute-done.8), channel_id=1, source_target_pairs={{0,4},{4,8},{8,12},{12,16},{16,20},{20,24},{24,28},{28,0},{1,5},{5... | collective-permute-start | bytes 393224 | tf_op jit(solution)/shard_map/ppermute | solution.py:18
  95.4 3.4 %copy-start.1 = (bf16[1024,2048]{1,0:T(8,128)(2,1)S(1)}, bf16[1024,2048]{1,0:T(8,128)(2,1)}, u32[]{:S(2)}) copy-start(bf16[1024,2048]{1,0:T(8,128)(2,1)} %get-tuple-element.54) | copy-start | bytes 12582916
  98.1 2.2 %copy-start = (bf16[1024,2048]{1,0:T(8,128)(2,1)S(1)}, bf16[1024,2048]{1,0:T(8,128)(2,1)}, u32[]{:S(2)}) copy-start(bf16[1024,2048]{1,0:T(8,128)(2,1)} %get-tuple-element.53) | copy-start | bytes 12582916
  100.3 6.3 %copy-start.3 = (s32[384,1]{0,1:T(1,128)S(1)}, s32[384,1]{0,1:T(1,128)}, u32[]{:S(2)}) copy-start(s32[384,1]{0,1:T(1,128)} %param.8) | copy-start | bytes 4612
  110.6 61.1 %all-to-all-start = ((s32[1,8,96]{2,0,1:T(1,128)}), s32[1,8,96]{2,0,1:T(1,128)S(1)}, u32[]{:S(2)}, u32[]{:S(2)}) async-start(s32[1,8,96]{2,0,1:T(1,128)} %all_to_all.14), calls=%async_computation | async-start | bytes 8192 | tf_op jit(solution)/shard_map/all_to_all | solution.py:85
  171.8 24.7 %all-to-all-start.1 = ((f32[512,8,96]{0,2,1:T(8,128)}), f32[512,8,96]{0,2,1:T(8,128)S(1)}, u32[]{:S(2)}, u32[]{:S(2)}) async-start(f32[512,8,96]{0,2,1:T(8,128)} %bitcast.39), calls=%async_computation.2 | async-start | bytes 3145728 | tf_op jit(solution)/shard_map/all_to_all | solution.py:84
Sparse Core Ops, SparseCore 0:
  106.7 60.5 reduce-scatter.1
where the time goes:
time: 205 us
  waiting for transfers between devices  117 us (57%)
  other arithmetic  42.5 us (21%)
  between operations  13.7 us (7%)
  local copies, waits for them, and re-layouts  13.5 us (7%)
  starting transfers between devices  10.2 us (5%)
  matrix products  7.49 us (4%)
    reduce_scatter x1, waiting for transfers between devices, on_device(): lax.psum_scatter(lax.dot_general(table, rows_all, (((0,), (1,)), ((), ())...  53.4 us
    ppermute x12, waiting for transfers between devices, from_behind(): lax.ppermute(array, axis, [(i, (i + by) % size) for i in range(size)])  44.1 us
    another operation x4, other arithmetic  36.3 us
    all_to_all x1, waiting for transfers between devices, on_device(): lax.all_to_all(outgoing, 'blk', split_axis=1, concat_axis=1, tiled=True)  19.8 us
    dot_general x1, matrix products, on_device(): lax.dot_general(table, rows_all, (((0,), (1,)), ((), ())), preferred_elem...  6.25 us
  transfers between devices with their start and end apart: 15, of which 12 were waited for; matrix products, arithmetic and copies ran while one was open for 25% of the time, Pallas kernels for 0%

commit v1 on v0

--- a/solution.py
+++ b/solution.py
@@ -1,16 +1,234 @@
+import functools
 import math
 
 import jax
 import jax.numpy as jnp
+import numpy as np
 from jax import lax
+from jax.experimental import pallas as pl
+from jax.experimental.pallas import tpu as pltpu
 from jax.sharding import PartitionSpec as P
 
 STA = 8
+WIN = 4
 BINS = 4096
 LAGS = 2048
 STEPS = 6
 SUB = 4
 VS_DEV = 16
+LANES = 128
+SPEC_ROWS = 2 * WIN * STA
+META_ROWS = 16
+
+VMEM = pl.BlockSpec(memory_space=pltpu.VMEM)
+
+
+def pack_kernel(spec_ref, weight_ref, mask_ref, owner_ref, local_ref, out_ref, plain):
+    dests = out_ref.shape[0]
+    for part in range(2):
+        for station in range(STA):
+            first = part * STA * WIN + station * WIN
+            values = spec_ref[part, station].astype(jnp.float32)
+            for dest in range(dests):
+                plain[dest, first : first + WIN, :] = values[:, dest * LANES : (dest + 1) * LANES]
+    for dest in range(dests):
+        for part in range(2):
+            for window in range(0, WIN, 2):
+                pair = [
+                    plain[dest, pl.ds(part * STA * WIN + window + more, STA, stride=WIN), :]
+                    for more in range(2)
+                ]
+                first = part * STA * WIN + window * STA
+                out_ref[dest, first : first + 2 * STA, :] = jnp.concatenate(pair, axis=0).astype(
+                    jnp.bfloat16
+                )
+    lane = lax.broadcasted_iota(jnp.int32, (1, LANES), 1)
+    owners, locals_ = [], []
+    for chunk in range(STEPS // 2):
+        part = slice(chunk * LANES, (chunk + 1) * LANES)
+        mask = jnp.zeros((1, LANES), jnp.int32)
+        for odd in range(2):
+            for near in range(2):
+                for far in range(2):
+                    here = (lane // 64 == odd) & (lane % 64 // 32 == near) & (lane % 8 // 4 == far)
+                    step = chunk * 2 + odd
+                    mask = jnp.where(here, mask_ref[near, far : far + 1, step : step + 1], mask)
+        owners.append(jnp.where(mask != 0, owner_ref[:, part], -1))
+        locals_.append(local_ref[:, part])
+    labels = jnp.concatenate(owners + locals_ + [jnp.zeros((2, LANES), jnp.int32)], axis=0)
+    station_of = lax.broadcasted_iota(jnp.int32, (STA, STA), 0)
+    on_lane = lax.broadcasted_iota(jnp.int32, (STA, STA), 1)
+    wide = lax.broadcasted_iota(jnp.int32, (STA, LANES), 1)
+    weights = jnp.zeros((STA, LANES), jnp.float32)
+    for window in range(WIN):
+        row = weight_ref[window : window + 1, :].astype(jnp.float32)
+        column = jnp.sum(jnp.where(station_of == on_lane, row, 0.0), axis=1, keepdims=True)
+        weights = jnp.where(wide == window, column, weights)
+    meta = jnp.concatenate([labels.astype(jnp.float32), weights], axis=0).astype(jnp.bfloat16)
+    for dest in range(dests):
+        out_ref[dest, SPEC_ROWS:, :] = meta
+
+
+def pack(spectra, quality, pair_mask, owners, local_rows, blocks):
+    rows = owners.shape[0]
+    return pl.pallas_call(
+        pack_kernel,
+        out_shape=jax.ShapeDtypeStruct((blocks, SPEC_ROWS + META_ROWS, LANES), jnp.bfloat16),
+        in_specs=[VMEM] * 5,
+        out_specs=VMEM,
+        scratch_shapes=[pltpu.VMEM((blocks, SPEC_ROWS, LANES), jnp.float32)],
+    )(
+        spectra,
+        quality.T,
+        pair_mask[0].transpose(1, 2, 0),
+        owners.reshape(1, rows),
+        local_rows.reshape(1, rows),
+    )
+
+
+def pair_kernel(got_ref, out_ref, spec, phat, total):
+    blocks = got_ref.shape[0]
+    groups = out_ref.shape[0] // blocks
+    sources = total.shape[0]
+
+    def weigh(block, carry):
+        weights = got_ref[block, SPEC_ROWS : SPEC_ROWS + META_ROWS, :].astype(jnp.float32)[STA:]
+        for first in range(0, SPEC_ROWS, 2 * STA):
+            both = got_ref[block, first : first + 2 * STA, :].astype(jnp.float32)
+            for more in range(2):
+                place = first // STA + more
+                window = place % WIN
+                column = weights[:, window : window + 1]
+                spec[block, place] = both[more * STA : (more + 1) * STA] * column
+        return carry
+
+    lax.fori_loop(0, blocks, weigh, 0)
+    total[...] = jnp.zeros_like(total)
+    source = lax.broadcasted_iota(jnp.int32, (sources, LANES), 0)
+
+    def correlate(block, carry):
+        for near in range(0, STA, 2):
+            own = [
+                [
+                    jnp.broadcast_to(spec[block, place, near + more : near + more + 1, :], (STA, LANES))
+                    for place in range(2 * WIN)
+                ]
+                for more in range(2)
+            ]
+            for step in range(STEPS):
+                far_block = lax.rem(block - 1 - step + blocks, blocks)
+                far = [spec[far_block, place] for place in range(2 * WIN)]
+                rows = []
+                for more in range(2):
+                    real, imag = 0.0, 0.0
+                    for window in range(WIN):
+                        a_real, a_imag = own[more][window], own[more][WIN + window]
+                        b_real, b_imag = far[window], far[WIN + window]
+                        real += a_real * b_real + a_imag * b_imag
+                        imag += a_imag * b_real - a_real * b_imag
+                    factor = lax.rsqrt(jnp.maximum(real * real + imag * imag, 1.0))
+                    rows.append((real * factor, imag * factor))
+                at = step * STA * STA + near * STA
+                for part in range(2):
+                    tile = jnp.concatenate([rows[0][part], rows[1][part]], axis=0)
+                    phat[at : at + 2 * STA, part * LANES : (part + 1) * LANES] = tile.astype(jnp.bfloat16)
+        names = got_ref[block, SPEC_ROWS : SPEC_ROWS + META_ROWS, :].astype(jnp.float32).astype(jnp.int32)
+        hots = []
+        for chunk in range(STEPS // 2):
+            label = names[chunk : chunk + 1] * VS_DEV + names[3 + chunk : 4 + chunk]
+            label = jnp.where(names[chunk : chunk + 1] < 0, -1, label)
+            hots.append((source == label).astype(jnp.bfloat16))
+        hot = jnp.concatenate(hots, axis=1)
+        total[...] += jnp.dot(hot, phat[...], preferred_element_type=jnp.float32)
+        return carry
+
+    lax.fori_loop(0, blocks, correlate, 0)
+    for block in range(blocks):
+        rows = total[block * VS_DEV : (block + 1) * VS_DEV, :].astype(jnp.bfloat16)
+        for group in range(groups):
+            out_ref[block * groups + group] = rows
+
+
+def pairs(got, groups):
+    blocks = got.shape[0]
+    return pl.pallas_call(
+        pair_kernel,
+        out_shape=jax.ShapeDtypeStruct((blocks * groups, VS_DEV, 2 * LANES), jnp.bfloat16),
+        in_specs=[VMEM],
+        out_specs=VMEM,
+        scratch_shapes=[
+            pltpu.VMEM((blocks, 2 * WIN, STA, LANES), jnp.float32),
+            pltpu.VMEM((STEPS * STA * STA, 2 * LANES), jnp.bfloat16),
+            pltpu.VMEM((blocks * VS_DEV, 2 * LANES), jnp.float32),
+        ],
+    )(got)
+
+
+def lag_kernel(bins_ref, wave_ref, turn_ref, out_ref, lags):
+    chunks = bins_ref.shape[0]
+    half = out_ref.shape[1]
+    rows = bins_ref[...].reshape(chunks * VS_DEV, 2 * LANES)
+    for column in range(0, 2 * half, 256):
+        part = slice(column, column + 256)
+        lags[:, part] = jnp.dot(rows, wave_ref[0, :, part], preferred_element_type=jnp.float32) + jnp.dot(
+            rows, wave_ref[1, :, part], preferred_element_type=jnp.float32
+        )
+    out_ref[...] = jnp.zeros_like(out_ref)
+
+    def add(chunk, carry):
+        at = pl.ds(pl.multiple_of(chunk * VS_DEV, VS_DEV), VS_DEV)
+        cosine, sine = turn_ref[0, pl.ds(chunk, 1), :], turn_ref[1, pl.ds(chunk, 1), :]
+        out_ref[...] += lags[at, :half] * cosine - lags[at, half:] * sine
+        return carry
+
+    lax.fori_loop(0, chunks, add, 0)
+
+
+def lags_of(bins, wave, turn):
+    half = wave.shape[2] // 2
+    return pl.pallas_call(
+        lag_kernel,
+        out_shape=jax.ShapeDtypeStruct((VS_DEV, half), jnp.float32),
+        in_specs=[VMEM] * 3,
+        out_specs=VMEM,
+        scratch_shapes=[pltpu.VMEM((bins.shape[0] * VS_DEV, 2 * half), jnp.float32)],
+    )(bins, wave, turn)
+
+
+def wave_table(first_lag, lag_dev):
+    bins = jnp.arange(LANES, dtype=jnp.int32)
+    shifts = first_lag + jnp.arange(lag_dev, dtype=jnp.int32)
+    phase = jnp.mod(bins[:, None] * shifts[None, :], 2 * BINS)
+    angle = phase.astype(jnp.float32) * (math.pi / BINS)
+    cosine, sine = jnp.cos(angle) / math.sqrt(BINS), jnp.sin(angle) / math.sqrt(BINS)
+    full = jnp.concatenate(
+        [jnp.concatenate([cosine, sine], axis=1), jnp.concatenate([-sine, cosine], axis=1)], axis=0
+    )
+    high = full.astype(jnp.bfloat16)
+    low = (full - high.astype(jnp.float32)).astype(jnp.bfloat16)
+    return jnp.stack([high, low])
+
+
+def turn_table(first_lag, lag_dev, blocks, groups):
+    places = jnp.arange(blocks * groups, dtype=jnp.int32)
+    chunk = places % groups * blocks + places // groups
+    shifts = first_lag + jnp.arange(lag_dev, dtype=jnp.int32)
+    phase = jnp.mod(LANES * chunk[:, None] * shifts[None, :], 2 * BINS)
+    angle = phase.astype(jnp.float32) * (math.pi / BINS)
+    return jnp.stack([jnp.cos(angle), jnp.sin(angle)])
+
+
+def by_bins(spectra, quality, pair_mask, owners, local_rows):
+    blocks, groups = lax.axis_size("blk"), lax.axis_size("grp")
+    lag_dev = LAGS // groups
+    first_lag = lax.axis_index("grp") * lag_dev - LAGS // 2
+    wave = wave_table(first_lag, lag_dev)
+    turn = turn_table(first_lag, lag_dev, blocks, groups)
+    sent = pack(spectra, quality, pair_mask, owners, local_rows, blocks)
+    got = lax.all_to_all(sent, "blk", split_axis=0, concat_axis=0, tiled=True)
+    summed = pairs(got, groups)
+    bins = lax.all_to_all(summed, ("blk", "grp"), split_axis=0, concat_axis=0, tiled=True)
+    return lags_of(bins, wave, turn)
 
 
 def from_behind(array, axis, by):
@@ -47,7 +265,7 @@
     return joined.reshape(STA * STA, joined.shape[2])
 
 
-def on_device(spectra, quality, pair_mask, owners, local_rows):
+def by_halo(spectra, quality, pair_mask, owners, local_rows):
     bins_dev = spectra.shape[3]
     blocks = lax.axis_size("blk")
     rows_dev = owners.shape[0]
@@ -95,6 +313,12 @@
     return stack
 
 
+def on_device(spectra, quality, pair_mask, owners, local_rows):
+    if spectra.shape[3] == lax.axis_size("blk") * LANES:
+        return by_bins(spectra, quality, pair_mask, owners, local_rows)
+    return by_halo(spectra, quality, pair_mask, owners, local_rows)
+
+
 def solution(mesh):
     in_specs = (
         P(None, "blk", None, "grp"),

time: 205 us -> 38.5 us (0.19)
  waiting for transfers between devices: 117 us -> 12.6 us
  other arithmetic: 42.5 us -> 3.41 us
  between operations: 13.7 us -> 0.06 us
  local copies, waits for them, and re-layouts: 13.5 us -> 2.61 us
  Pallas kernels: 0 us -> 10.3 us
  matrix products: 7.49 us -> 0 us
    reduce_scatter x1 -> x0, waiting for transfers between devices: 53.4 us -> none  [on_device(): lax.psum_scatter(lax.dot_general(table, rows_all, (((0,), (1,)), ((), ())...]
    ppermute x12 -> x0, waiting for transfers between devices: 44.1 us -> none  [from_behind(): lax.ppermute(array, axis, [(i, (i + by) % size) for i in range(size)])]
    another operation x4 -> x2, other arithmetic: 36.3 us -> 1.74 us  [the longest x1 1.06 us: wave_table(): return jnp.stack([high, low])]
    pallas_call x0 -> x3, Pallas kernels: none -> 10.3 us  [the longest x1 5.55 us: pairs(): pl.pallas_call(pair_kernel, out_shape=jax.ShapeDtypeStruct((blocks * grou...]
    dot_general x2 -> x0, matrix products: 7.49 us -> none  [the longest x1 6.25 us: on_device(): lax.dot_general(table, rows_all, (((0,), (1,)), ((), ())), preferred_elem...]
    all_to_all x2, waiting for transfers between devices: 19.8 us -> 12.6 us  [the longest x1 8.17 us: by_bins(): lax.all_to_all(summed, ('blk', 'grp'), split_axis=0, concat_axis=0, tiled...]
    scatter x2 -> x0, local copies, waits for them, and re-layouts: 6.12 us -> none  [the longest x1 3.08 us: on_device(): jnp.full((1, blocks * capacity), -1, jnp.int32).at[0, slot_index]]
    ppermute x12 -> x0, starting transfers between devices: 3.2 us -> none  [from_behind(): lax.ppermute(array, axis, [(i, (i + by) % size) for i in range(size)])]
  transfers between devices with their start and end apart: 15 -> 2, of which waited for: 12 -> 2; matrix products, arithmetic and copies ran while one was open for 25% -> 9% of each run, Pallas kernels for 0% -> 0%
where the time goes in v1:
time: 38.5 us; the launch traced here: 38.2 us
  waiting for transfers between devices  12.6 us (33%)
  Pallas kernels  10.3 us (27%)
  starting transfers between devices  9.14 us (24%)
  other arithmetic  3.41 us (9%)
  local copies, waits for them, and re-layouts  2.61 us (7%)
    all_to_all x1, waiting for transfers between devices, by_bins(): lax.all_to_all(summed, ('blk', 'grp'), split_axis=0, concat_axis=0, tiled...  8.17 us
    pallas_call x1, Pallas kernels, pairs(): pl.pallas_call(pair_kernel, out_shape=jax.ShapeDtypeStruct((blocks * grou...  5.55 us
    all_to_all x1, starting transfers between devices, by_bins(): got = lax.all_to_all(sent, 'blk', split_axis=0, concat_axis=0, tiled=True)  5.17 us
    all_to_all x1, waiting for transfers between devices, by_bins(): got = lax.all_to_all(sent, 'blk', split_axis=0, concat_axis=0, tiled=True)  4.45 us
    all_to_all x1, starting transfers between devices, by_bins(): lax.all_to_all(summed, ('blk', 'grp'), split_axis=0, concat_axis=0, tiled...  3.97 us
    pallas_call x1, Pallas kernels, lags_of(): pl.pallas_call(lag_kernel, out_shape=jax.ShapeDtypeStruct((VS_DEV, half),...  3.08 us
    pallas_call x1, Pallas kernels, pack(): pl.pallas_call(pack_kernel, out_shape=jax.ShapeDtypeStruct((blocks, SPEC_...  1.73 us
    unnamed x4, local copies, waits for them, and re-layouts  1.36 us
  transfers between devices with their start and end apart: 2, of which 2 were waited for; matrix products, arithmetic and copies ran while one was open for 9% of the time, Pallas kernels for 0%

profile of v1, /device:TPU:0, one launch (start us, length us, event | category | flops | bytes accessed | tf_op | source)
XLA Modules:
  0.0 38.2 jit_solution(16634185565369753962)
XLA Ops:
  0.0 1.2 %reshape.233.local_ref = s32[1,384]{1,0:T(1,128)} reshape(s32[384]{0:T(512)} %param.9) | data formatting | bytes 3072 | tf_op jit(solution)/shard_map/reshape | solution.py:85
  1.2 1.7 %shard_map.55 = bf16[8,80,128]{2,1,0:T(8,128)(2,1)} custom-call(bf16[2,8,4,1024]{3,2,1,0:T(4,128)(2,1)} %spec_ref.1, s32[4,8]{1,0:T(4,128)} %bitcast.9, s32[2,2,6]{2,1,0:T(2,128)} %bitcast.10, s32[1,384]{1,0:T(1,128)} %bitcast.11, s32[1,384]{1,0:T(1,128)} %reshape.233.local_ref), custom_call_target="tpu_custom_call" | custom-call | tf_op jit(solution)/shard_map/pallas_call | solution.py:74
  3.0 5.2 %all-to-all-start = ((bf16[8,80,128]{2,1,0:T(8,128)(2,1)}), bf16[8,80,128]{2,1,0:T(8,128)(2,1)S(1)}, u32[]{:S(2)}, u32[]{:S(2)}) async-start(bf16[8,80,128]{2,1,0:T(8,128)(2,1)} %shard_map.55), calls=%async_computation | async-start | bytes 327680 | tf_op jit(solution)/shard_map/all_to_all | solution.py:228
  8.2 1.1 %sine_multiply_fusion = (f32[128,512]{1,0:T(8,128)S(1)}, f32[128,512]{1,0:T(8,128)S(1)}, f32[128,512]{1,0:T(8,128)S(1)}) fusion(s32[512]{0:T(512)S(1)} %iota_add_fusion), kind=kLoop, calls=%fused_computation.12 | loop fusion | flops 1114112 | bytes 788480 | tf_op jit(solution)/shard_map/div | solution.py:203
  9.2 0.3 fusion.12
  9.6 4.5 %all-to-all-done.got_ref = bf16[8,80,128]{2,1,0:T(8,128)(2,1)S(1)} async-done(((bf16[8,80,128]{2,1,0:T(8,128)(2,1)}), bf16[8,80,128]{2,1,0:T(8,128)(2,1)S(1)}, u32[]{:S(2)}, u32[]{:S(2)}) %all-to-all-start) | async-done | bytes 163872 | tf_op jit(solution)/shard_map/all_to_all | solution.py:228
  14.0 0.0 copy-start.1
  14.0 0.6 %copy-done.1 = bf16[8,80,128]{2,1,0:T(8,128)(2,1)} copy-done((bf16[8,80,128]{2,1,0:T(8,128)(2,1)}, bf16[8,80,128]{2,1,0:T(8,128)(2,1)S(1)}, u32[]{:S(2)}) %copy-start.1) | copy-done | bytes 163864
  14.7 5.5 %shard_map.56 = bf16[32,16,256]{2,1,0:T(8,128)(2,1)} custom-call(bf16[8,80,128]{2,1,0:T(8,128)(2,1)} %copy-done.1), custom_call_target="tpu_custom_call" | custom-call | tf_op jit(solution)/shard_map/pallas_call | solution.py:154
  20.2 4.0 %all-to-all-start.1 = ((bf16[32,16,256]{2,1,0:T(8,128)(2,1)}), bf16[32,16,256]{2,1,0:T(8,128)(2,1)S(1)}, u32[]{:S(2)}, u32[]{:S(2)}) async-start(bf16[32,16,256]{2,1,0:T(8,128)(2,1)} %shard_map.56), calls=%async_computation.1 | async-start | bytes 524288 | tf_op jit(solution)/shard_map/all_to_all | solution.py:230
  24.2 0.1 maximum_bitcast_fusion
  24.3 0.7 %pad_maximum_fusion.2.turn_ref = f32[2,32,512]{2,1,0:T(8,128)} fusion(f32[1,32,512]{2,1,0:T(8,128)S(1)} %get-tuple-element.8, f32[1,32,512]{2,1,0:T(8,128)S(1)} %get-tuple-element.7), kind=kLoop, calls=%fused_computation.17 | loop fusion | flops 32768 | bytes 262144 | tf_op jit(solution)/shard_map/stack | solution.py:218
  25.0 0.1 fusion
  25.1 0.1 subtract_convert_fusion
  25.2 1.1 %pad_maximum_fusion.1.wave_ref = bf16[2,256,1024]{2,1,0:T(8,128)(2,1)} fusion(bf16[1,256,1024]{2,1,0:T(8,128)(2,1)S(1)} %subtract_convert_fusion, bf16[1,256,1024]{2,1,0:T(8,128)(2,1)S(1)} %fusion), kind=kLoop, calls=%fused_computation.1 | loop fusion | flops 524288 | bytes 2097152 | tf_op jit(solution)/shard_map/stack | solution.py:209
  26.2 8.2 %all-to-all-done.1.bins_ref = bf16[32,16,256]{2,1,0:T(8,128)(2,1)S(1)} async-done(((bf16[32,16,256]{2,1,0:T(8,128)(2,1)}), bf16[32,16,256]{2,1,0:T(8,128)(2,1)S(1)}, u32[]{:S(2)}, u32[]{:S(2)}) %all-to-all-start.1) | async-done | bytes 262176 | tf_op jit(solution)/shard_map/all_to_all | solution.py:230
  34.4 0.0 copy-start
  34.4 0.7 %copy-done = bf16[32,16,256]{2,1,0:T(8,128)(2,1)} copy-done((bf16[32,16,256]{2,1,0:T(8,128)(2,1)}, bf16[32,16,256]{2,1,0:T(8,128)(2,1)S(1)}, u32[]{:S(2)}) %copy-start) | copy-done | bytes 262168
  35.1 3.1 %shard_map.57 = f32[16,512]{1,0:T(8,128)} custom-call(bf16[32,16,256]{2,1,0:T(8,128)(2,1)} %copy-done, bf16[2,256,1024]{2,1,0:T(8,128)(2,1)} %pad_maximum_fusion.1.wave_ref, f32[2,32,512]{2,1,0:T(8,128)} %pad_maximum_fusion.2.turn_ref), custom_call_target="tpu_custom_call" | custom-call | tf_op jit(solution)/shard_map/pallas_call | solution.py:189
  (2 shorter events, 0.0 us)
Async XLA Ops:
  3.0 11.1 %all-to-all-start = ((bf16[8,80,128]{2,1,0:T(8,128)(2,1)}), bf16[8,80,128]{2,1,0:T(8,128)(2,1)S(1)}, u32[]{:S(2)}, u32[]{:S(2)}) async-start(bf16[8,80,128]{2,1,0:T(8,128)(2,1)} %shard_map.55), calls=%async_computation | async-start | bytes 327680 | tf_op jit(solution)/shard_map/all_to_all | solution.py:228
  14.0 0.7 %copy-start.1 = (bf16[8,80,128]{2,1,0:T(8,128)(2,1)}, bf16[8,80,128]{2,1,0:T(8,128)(2,1)S(1)}, u32[]{:S(2)}) copy-start(bf16[8,80,128]{2,1,0:T(8,128)(2,1)S(1)} %all-to-all-done.got_ref) | copy-start | bytes 491524
  20.2 14.2 %all-to-all-start.1 = ((bf16[32,16,256]{2,1,0:T(8,128)(2,1)}), bf16[32,16,256]{2,1,0:T(8,128)(2,1)S(1)}, u32[]{:S(2)}, u32[]{:S(2)}) async-start(bf16[32,16,256]{2,1,0:T(8,128)(2,1)} %shard_map.56), calls=%async_computation.1 | async-start | bytes 524288 | tf_op jit(solution)/shard_map/all_to_all | solution.py:230
  34.4 0.7 %copy-start = (bf16[32,16,256]{2,1,0:T(8,128)(2,1)}, bf16[32,16,256]{2,1,0:T(8,128)(2,1)S(1)}, u32[]{:S(2)}) copy-start(bf16[32,16,256]{2,1,0:T(8,128)(2,1)S(1)} %all-to-all-done.1.bins_ref) | copy-start | bytes 786436

commit v2 on v1

--- a/solution.py
+++ b/solution.py
@@ -19,12 +19,29 @@
 LANES = 128
 SPEC_ROWS = 2 * WIN * STA
 META_ROWS = 16
+KERNEL_VMEM = 12 * 1024 * 1024
 
 VMEM = pl.BlockSpec(memory_space=pltpu.VMEM)
 
 
-def pack_kernel(spec_ref, weight_ref, mask_ref, owner_ref, local_ref, out_ref, plain):
+def pack_kernel(spec_hbm, weight_hbm, mask_hbm, owner_hbm, local_hbm, out_ref, spec_ref, weight_ref, mask_ref, owner_ref, local_ref, plain, arrived):
     dests = out_ref.shape[0]
+    moves = [
+        pltpu.make_async_copy(source, target, arrived.at[place])
+        for place, (source, target) in enumerate(
+            [
+                (spec_hbm, spec_ref),
+                (weight_hbm, weight_ref),
+                (mask_hbm, mask_ref),
+                (owner_hbm, owner_ref),
+                (local_hbm, local_ref),
+            ]
+        )
+    ]
+    for move in moves:
+        move.start()
+    for move in moves:
+        move.wait()
     for part in range(2):
         for station in range(STA):
             first = part * STA * WIN + station * WIN
@@ -54,7 +71,7 @@
                     step = chunk * 2 + odd
                     mask = jnp.where(here, mask_ref[near, far : far + 1, step : step + 1], mask)
         owners.append(jnp.where(mask != 0, owner_ref[:, part], -1))
-        locals_.append(local_ref[:, part])
+        locals_.append(local_ref[part].reshape(1, LANES))
     labels = jnp.concatenate(owners + locals_ + [jnp.zeros((2, LANES), jnp.int32)], axis=0)
     station_of = lax.broadcasted_iota(jnp.int32, (STA, STA), 0)
     on_lane = lax.broadcasted_iota(jnp.int32, (STA, STA), 1)
@@ -71,19 +88,25 @@
 
 def pack(spectra, quality, pair_mask, owners, local_rows, blocks):
     rows = owners.shape[0]
-    return pl.pallas_call(
-        pack_kernel,
-        out_shape=jax.ShapeDtypeStruct((blocks, SPEC_ROWS + META_ROWS, LANES), jnp.bfloat16),
-        in_specs=[VMEM] * 5,
-        out_specs=VMEM,
-        scratch_shapes=[pltpu.VMEM((blocks, SPEC_ROWS, LANES), jnp.float32)],
-    )(
+    operands = (
         spectra,
         quality.T,
         pair_mask[0].transpose(1, 2, 0),
         owners.reshape(1, rows),
-        local_rows.reshape(1, rows),
-    )
+        local_rows,
+    )
+    return pl.pallas_call(
+        pack_kernel,
+        out_shape=pltpu.VMEM((blocks, SPEC_ROWS + META_ROWS, LANES), jnp.bfloat16),
+        in_specs=[pl.BlockSpec(memory_space=pltpu.HBM)] * len(operands),
+        out_specs=VMEM,
+        compiler_params=pltpu.CompilerParams(vmem_limit_bytes=KERNEL_VMEM),
+        scratch_shapes=[pltpu.VMEM(each.shape, each.dtype) for each in operands]
+        + [
+            pltpu.VMEM((blocks, SPEC_ROWS, LANES), jnp.float32),
+            pltpu.SemaphoreType.DMA((len(operands),)),
+        ],
+    )(*[pltpu.with_memory_space_constraint(each, pltpu.HBM) for each in operands])
 
 
 def pair_kernel(got_ref, out_ref, spec, phat, total):
@@ -153,9 +176,10 @@
     blocks = got.shape[0]
     return pl.pallas_call(
         pair_kernel,
-        out_shape=jax.ShapeDtypeStruct((blocks * groups, VS_DEV, 2 * LANES), jnp.bfloat16),
+        out_shape=pltpu.VMEM((blocks * groups, VS_DEV, 2 * LANES), jnp.bfloat16),
         in_specs=[VMEM],
         out_specs=VMEM,
+        compiler_params=pltpu.CompilerParams(vmem_limit_bytes=KERNEL_VMEM),
         scratch_shapes=[
             pltpu.VMEM((blocks, 2 * WIN, STA, LANES), jnp.float32),
             pltpu.VMEM((STEPS * STA * STA, 2 * LANES), jnp.bfloat16),
@@ -191,6 +215,7 @@
         out_shape=jax.ShapeDtypeStruct((VS_DEV, half), jnp.float32),
         in_specs=[VMEM] * 3,
         out_specs=VMEM,
+        compiler_params=pltpu.CompilerParams(vmem_limit_bytes=KERNEL_VMEM),
         scratch_shapes=[pltpu.VMEM((bins.shape[0] * VS_DEV, 2 * half), jnp.float32)],
     )(bins, wave, turn)
 
@@ -226,6 +251,7 @@
     turn = turn_table(first_lag, lag_dev, blocks, groups)
     sent = pack(spectra, quality, pair_mask, owners, local_rows, blocks)
     got = lax.all_to_all(sent, "blk", split_axis=0, concat_axis=0, tiled=True)
+    got, wave, turn = lax.optimization_barrier((got, wave, turn))
     summed = pairs(got, groups)
     bins = lax.all_to_all(summed, ("blk", "grp"), split_axis=0, concat_axis=0, tiled=True)
     return lags_of(bins, wave, turn)

time: 38.5 us -> 32.7 us (0.85)
  blocking collectives: 0 us -> 14 us
  waiting for transfers between devices: 12.6 us -> 4.04 us
  starting transfers between devices: 9.14 us -> 5.18 us
  Pallas kernels: 10.3 us -> 7.43 us
  local copies, waits for them, and re-layouts: 2.61 us -> 0 us
  other arithmetic: 3.41 us -> 1.78 us
    all_to_all x0 -> x1, blocking collectives: none -> 14 us  [by_bins(): lax.all_to_all(summed, ('blk', 'grp'), split_axis=0, concat_axis=0, tiled...]
    all_to_all x1 -> x0, waiting for transfers between devices: 8.17 us -> none  [by_bins(): lax.all_to_all(summed, ('blk', 'grp'), split_axis=0, concat_axis=0, tiled...]
    all_to_all x1 -> x0, starting transfers between devices: 3.97 us -> none  [by_bins(): lax.all_to_all(summed, ('blk', 'grp'), split_axis=0, concat_axis=0, tiled...]
    pallas_call x2, Pallas kernels: 7.27 us -> 5.66 us  [the longest x1 3.91 us: pairs(): pl.pallas_call(pair_kernel, out_shape=pltpu.VMEM((blocks * groups, VS_DEV...]
    unnamed x4 -> x0, local copies, waits for them, and re-layouts: 1.36 us -> none
    pallas_call x1, Pallas kernels: 3.08 us -> 1.78 us  [lags_of(): pl.pallas_call(lag_kernel, out_shape=jax.ShapeDtypeStruct((VS_DEV, half),...]
    reshape x1 -> x0, local copies, waits for them, and re-layouts: 1.24 us -> none  [pack(): local_rows.reshape(1, rows)]
    another operation x1, other arithmetic: 1.06 us -> 0.1 us  [wave_table(): return jnp.stack([high, low])]
  transfers between devices with their start and end apart: 2 -> 1, of which waited for: 2 -> 1; matrix products, arithmetic and copies ran while one was open for 9% -> 5% of each run, Pallas kernels for 0% -> 0%
where the time goes in v2:
time: 32.7 us; the launch traced here: 32.5 us
  blocking collectives  14 us (43%)
  Pallas kernels  7.43 us (23%)
  starting transfers between devices  5.18 us (16%)
  waiting for transfers between devices  4.04 us (12%)
  other arithmetic  1.78 us (5%)
    all_to_all x1, blocking collectives, by_bins(): lax.all_to_all(summed, ('blk', 'grp'), split_axis=0, concat_axis=0, tiled...  14 us
    all_to_all x1, starting transfers between devices, by_bins(): got = lax.all_to_all(sent, 'blk', split_axis=0, concat_axis=0, tiled=True)  5.18 us
    all_to_all x1, waiting for transfers between devices, by_bins(): got = lax.all_to_all(sent, 'blk', split_axis=0, concat_axis=0, tiled=True)  4.04 us
    pallas_call x1, Pallas kernels, pairs(): pl.pallas_call(pair_kernel, out_shape=pltpu.VMEM((blocks * groups, VS_DEV...  3.91 us
    pallas_call x1, Pallas kernels, lags_of(): pl.pallas_call(lag_kernel, out_shape=jax.ShapeDtypeStruct((VS_DEV, half),...  1.78 us
    pallas_call x1, Pallas kernels, pack(): pl.pallas_call(pack_kernel, out_shape=pltpu.VMEM((blocks, SPEC_ROWS + MET...  1.75 us
    div x1, other arithmetic, wave_table(): jnp.sin(angle) / math.sqrt(BINS)  1.06 us
  transfers between devices with their start and end apart: 1, of which 1 were waited for; matrix products, arithmetic and copies ran while one was open for 5% of the time, Pallas kernels for 0%

profile of v2, /device:TPU:0, one launch (start us, length us, event | category | flops | bytes accessed | tf_op | source)
XLA Modules:
  0.0 32.5 jit_solution(15297065864284068787)
XLA Ops:
  0.0 1.7 %shard_map.55 = bf16[8,80,128]{2,1,0:T(8,128)(2,1)} custom-call(bf16[2,8,4,1024]{3,2,1,0:T(4,128)(2,1)} %spec_hbm.1, s32[4,8]{1,0:T(4,128)} %bitcast.9, s32[2,2,6]{2,1,0:T(2,128)} %bitcast.10, s32[1,384]{1,0:T(1,128)} %bitcast.11, s32[384]{0:T(512)} %local_hbm.1), custom_call_target="tpu_custom_call" | custom-call | tf_op jit(solution)/shard_map/pallas_call | solution.py:98
  1.8 5.2 %all-to-all-start = ((bf16[8,80,128]{2,1,0:T(8,128)(2,1)}), bf16[8,80,128]{2,1,0:T(8,128)(2,1)S(1)}, u32[]{:S(2)}, u32[]{:S(2)}) async-start(bf16[8,80,128]{2,1,0:T(8,128)(2,1)} %shard_map.55), calls=%async_computation | async-start | bytes 327680 | tf_op jit(solution)/shard_map/all_to_all | solution.py:253
  6.9 1.1 %sine_multiply_fusion = (f32[128,512]{1,0:T(8,128)S(1)}, f32[128,512]{1,0:T(8,128)S(1)}, f32[128,512]{1,0:T(8,128)S(1)}) fusion(s32[512]{0:T(512)S(1)} %iota_add_fusion), kind=kLoop, calls=%fused_computation.12 | loop fusion | flops 1114112 | bytes 788480 | tf_op jit(solution)/shard_map/div | solution.py:228
  8.0 0.1 maximum_bitcast_fusion
  8.1 0.1 fusion
  8.2 0.1 subtract_convert_fusion
  8.3 0.3 %fusion.12 = (f32[1,32,512]{2,1,0:T(8,128)S(1)}, f32[1,32,512]{2,1,0:T(8,128)S(1)}) fusion(s32[512]{0:T(512)S(1)} %iota_add_fusion, s32[32]{0:T(128)S(1)} %fusion.15), kind=kLoop, calls=%fused_computation.28 | loop fusion | flops 229376 | bytes 133248 | tf_op jit(solution)/shard_map/cos | solution.py:243
  8.7 0.1 pad_maximum_fusion.1.wave_ref
  8.8 4.0 %all-to-all-done.got_ref = bf16[8,80,128]{2,1,0:T(8,128)(2,1)S(1)} async-done(((bf16[8,80,128]{2,1,0:T(8,128)(2,1)}), bf16[8,80,128]{2,1,0:T(8,128)(2,1)S(1)}, u32[]{:S(2)}, u32[]{:S(2)}) %all-to-all-start) | async-done | bytes 163872 | tf_op jit(solution)/shard_map/all_to_all | solution.py:253
  12.8 3.9 %shard_map.56 = bf16[32,16,256]{2,1,0:T(8,128)(2,1)S(1)} custom-call(bf16[8,80,128]{2,1,0:T(8,128)(2,1)S(1)} %all-to-all-done.got_ref), custom_call_target="tpu_custom_call" | custom-call | tf_op jit(solution)/shard_map/pallas_call | solution.py:177
  16.7 14.0 %all_to_all.10.bins_ref = bf16[32,16,256]{2,1,0:T(8,128)(2,1)S(1)} all-to-all(bf16[32,16,256]{2,1,0:T(8,128)(2,1)S(1)} %shard_map.56), channel_id=1, replica_groups=mesh['blk'=8,'grp'=4] {'blk','grp'}, dimensions={0} | all-to-all | bytes 524288 | tf_op jit(solution)/shard_map/all_to_all | solution.py:256
  30.7 1.8 %shard_map.57 = f32[16,512]{1,0:T(8,128)} custom-call(bf16[32,16,256]{2,1,0:T(8,128)(2,1)S(1)} %all_to_all.10.bins_ref, bf16[2,256,1024]{2,1,0:T(8,128)(2,1)S(1)} %pad_maximum_fusion.1.wave_ref, f32[2,32,512]{2,1,0:T(8,128)S(1)} %pad_maximum_fusion.2.turn_ref), custom_call_target="tpu_custom_call" | custom-call | tf_op jit(solution)/shard_map/pallas_call | solution.py:213
  (3 shorter events, 0.0 us)
Async XLA Ops:
  1.8 11.1 %all-to-all-start = ((bf16[8,80,128]{2,1,0:T(8,128)(2,1)}), bf16[8,80,128]{2,1,0:T(8,128)(2,1)S(1)}, u32[]{:S(2)}, u32[]{:S(2)}) async-start(bf16[8,80,128]{2,1,0:T(8,128)(2,1)} %shard_map.55), calls=%async_computation | async-start | bytes 327680 | tf_op jit(solution)/shard_map/all_to_all | solution.py:253

commit v3 on v2

--- a/solution.py
+++ b/solution.py
@@ -24,7 +24,21 @@
 VMEM = pl.BlockSpec(memory_space=pltpu.VMEM)
 
 
-def pack_kernel(spec_hbm, weight_hbm, mask_hbm, owner_hbm, local_hbm, out_ref, spec_ref, weight_ref, mask_ref, owner_ref, local_ref, plain, arrived):
+def pack_kernel(
+    spec_hbm,
+    weight_hbm,
+    mask_hbm,
+    owner_hbm,
+    local_hbm,
+    out_ref,
+    spec_ref,
+    weight_ref,
+    mask_ref,
+    owner_ref,
+    local_ref,
+    plain,
+    arrived,
+):
     dests = out_ref.shape[0]
     moves = [
         pltpu.make_async_copy(source, target, arrived.at[place])
@@ -40,6 +54,11 @@
     ]
     for move in moves:
         move.start()
+    lane = lax.broadcasted_iota(jnp.int32, (1, LANES), 1)
+    lane_in = lax.broadcasted_iota(jnp.int32, (LANES, LANES), 0)
+    lane_out = lax.broadcasted_iota(jnp.int32, (LANES, LANES), 1)
+    turned = lane_out // 64 * 64 + lane_out % STA * STA + lane_out % 64 // STA
+    swap = (lane_in == turned).astype(jnp.float32).astype(jnp.bfloat16)
     for move in moves:
         move.wait()
     for part in range(2):
@@ -48,6 +67,29 @@
             values = spec_ref[part, station].astype(jnp.float32)
             for dest in range(dests):
                 plain[dest, first : first + WIN, :] = values[:, dest * LANES : (dest + 1) * LANES]
+    labels = []
+    for chunk in range(STEPS // 2):
+        part = slice(chunk * LANES, (chunk + 1) * LANES)
+        mask = jnp.zeros((1, LANES), jnp.int32)
+        for odd in range(2):
+            for near in range(2):
+                for far in range(2):
+                    here = (lane // 64 == odd) & (lane % 64 // 32 == near) & (lane % 8 // 4 == far)
+                    step = chunk * 2 + odd
+                    mask = jnp.where(here, mask_ref[near, far : far + 1, step : step + 1], mask)
+        source = owner_ref[:, part] * VS_DEV + local_ref[part].reshape(1, LANES)
+        labels.append(jnp.where(mask != 0, source, -1).astype(jnp.float32))
+    last = jnp.broadcast_to(labels[2], (STA, LANES)).astype(jnp.bfloat16)
+    labels[2] = jnp.dot(last, swap, preferred_element_type=jnp.float32)[:1]
+    station_of = lax.broadcasted_iota(jnp.int32, (STA, STA), 0)
+    on_lane = lax.broadcasted_iota(jnp.int32, (STA, STA), 1)
+    wide = lax.broadcasted_iota(jnp.int32, (STA, LANES), 1)
+    weights = jnp.zeros((STA, LANES), jnp.float32)
+    for window in range(WIN):
+        row = weight_ref[window : window + 1, :].astype(jnp.float32)
+        column = jnp.sum(jnp.where(station_of == on_lane, row, 0.0), axis=1, keepdims=True)
+        weights = jnp.where(wide == window, column, weights)
+    meta = jnp.concatenate(labels + [jnp.zeros((5, LANES), jnp.float32), weights], axis=0).astype(jnp.bfloat16)
     for dest in range(dests):
         for part in range(2):
             for window in range(0, WIN, 2):
@@ -59,30 +101,6 @@
                 out_ref[dest, first : first + 2 * STA, :] = jnp.concatenate(pair, axis=0).astype(
                     jnp.bfloat16
                 )
-    lane = lax.broadcasted_iota(jnp.int32, (1, LANES), 1)
-    owners, locals_ = [], []
-    for chunk in range(STEPS // 2):
-        part = slice(chunk * LANES, (chunk + 1) * LANES)
-        mask = jnp.zeros((1, LANES), jnp.int32)
-        for odd in range(2):
-            for near in range(2):
-                for far in range(2):
-                    here = (lane // 64 == odd) & (lane % 64 // 32 == near) & (lane % 8 // 4 == far)
-                    step = chunk * 2 + odd
-                    mask = jnp.where(here, mask_ref[near, far : far + 1, step : step + 1], mask)
-        owners.append(jnp.where(mask != 0, owner_ref[:, part], -1))
-        locals_.append(local_ref[part].reshape(1, LANES))
-    labels = jnp.concatenate(owners + locals_ + [jnp.zeros((2, LANES), jnp.int32)], axis=0)
-    station_of = lax.broadcasted_iota(jnp.int32, (STA, STA), 0)
-    on_lane = lax.broadcasted_iota(jnp.int32, (STA, STA), 1)
-    wide = lax.broadcasted_iota(jnp.int32, (STA, LANES), 1)
-    weights = jnp.zeros((STA, LANES), jnp.float32)
-    for window in range(WIN):
-        row = weight_ref[window : window + 1, :].astype(jnp.float32)
-        column = jnp.sum(jnp.where(station_of == on_lane, row, 0.0), axis=1, keepdims=True)
-        weights = jnp.where(wide == window, column, weights)
-    meta = jnp.concatenate([labels.astype(jnp.float32), weights], axis=0).astype(jnp.bfloat16)
-    for dest in range(dests):
         out_ref[dest, SPEC_ROWS:, :] = meta
 
 
@@ -109,27 +127,34 @@
     )(*[pltpu.with_memory_space_constraint(each, pltpu.HBM) for each in operands])
 
 
-def pair_kernel(got_ref, out_ref, spec, phat, total):
+def pair_kernel(got_ref, lead_ref, out_ref, spec, phat, hot, total):
     blocks = got_ref.shape[0]
     groups = out_ref.shape[0] // blocks
-    sources = total.shape[0]
-
-    def weigh(block, carry):
+    sources = blocks * VS_DEV
+    kept = STEPS // 2 + 1
+    block_rows = kept * STA * STA
+
+    for block in range(blocks):
         weights = got_ref[block, SPEC_ROWS : SPEC_ROWS + META_ROWS, :].astype(jnp.float32)[STA:]
+        columns = [weights[:, window : window + 1] for window in range(WIN)]
         for first in range(0, SPEC_ROWS, 2 * STA):
             both = got_ref[block, first : first + 2 * STA, :].astype(jnp.float32)
             for more in range(2):
                 place = first // STA + more
-                window = place % WIN
-                column = weights[:, window : window + 1]
-                spec[block, place] = both[more * STA : (more + 1) * STA] * column
-        return carry
-
-    lax.fori_loop(0, blocks, weigh, 0)
-    total[...] = jnp.zeros_like(total)
-    source = lax.broadcasted_iota(jnp.int32, (sources, LANES), 0)
+                spec[block, place] = both[more * STA : (more + 1) * STA] * columns[place % WIN]
+
+    source = lax.broadcasted_iota(jnp.int32, (sources, LANES), 0).astype(jnp.float32)
+    lane = lax.broadcasted_iota(jnp.int32, (1, LANES), 1)
+
+    def earlier(block, by):
+        return lax.rem(block - by + blocks, blocks)
+
+    def names(block, chunk):
+        rows = got_ref[block, SPEC_ROWS : SPEC_ROWS + META_ROWS, :].astype(jnp.float32)
+        return rows[chunk : chunk + 1]
 
     def correlate(block, carry):
+        base = pl.multiple_of(block * block_rows, block_rows)
         for near in range(0, STA, 2):
             own = [
                 [
@@ -138,8 +163,8 @@
                 ]
                 for more in range(2)
             ]
-            for step in range(STEPS):
-                far_block = lax.rem(block - 1 - step + blocks, blocks)
+            for step in range(kept):
+                far_block = earlier(block, 1 + step)
                 far = [spec[far_block, place] for place in range(2 * WIN)]
                 rows = []
                 for more in range(2):
@@ -151,108 +176,110 @@
                         imag += a_imag * b_real - a_real * b_imag
                     factor = lax.rsqrt(jnp.maximum(real * real + imag * imag, 1.0))
                     rows.append((real * factor, imag * factor))
-                at = step * STA * STA + near * STA
+                at = base + (step * STA * STA + near * STA)
                 for part in range(2):
                     tile = jnp.concatenate([rows[0][part], rows[1][part]], axis=0)
-                    phat[at : at + 2 * STA, part * LANES : (part + 1) * LANES] = tile.astype(jnp.bfloat16)
-        names = got_ref[block, SPEC_ROWS : SPEC_ROWS + META_ROWS, :].astype(jnp.float32).astype(jnp.int32)
-        hots = []
-        for chunk in range(STEPS // 2):
-            label = names[chunk : chunk + 1] * VS_DEV + names[3 + chunk : 4 + chunk]
-            label = jnp.where(names[chunk : chunk + 1] < 0, -1, label)
-            hots.append((source == label).astype(jnp.bfloat16))
-        hot = jnp.concatenate(hots, axis=1)
-        total[...] += jnp.dot(hot, phat[...], preferred_element_type=jnp.float32)
+                    phat[pl.ds(pl.multiple_of(at, 2 * STA), 2 * STA), part * LANES : (part + 1) * LANES] = (
+                        tile.astype(jnp.bfloat16)
+                    )
+        again = [
+            jnp.where(lane >= LANES // 2, names(earlier(block, 2), 2), -1.0),
+            jnp.where(lane < LANES // 2, names(earlier(block, 3), 2), -1.0),
+        ]
+        for chunk in range(2):
+            forth = (source == names(block, chunk)).astype(jnp.float32)
+            back = (source == again[chunk]).astype(jnp.float32)
+            at = pl.ds(pl.multiple_of(base + chunk * LANES, LANES), LANES)
+            hot[:sources, at] = (forth + back).astype(jnp.bfloat16)
+            hot[sources:, at] = (forth - back).astype(jnp.bfloat16)
         return carry
 
     lax.fori_loop(0, blocks, correlate, 0)
+    total[...] = jnp.dot(hot[...], phat[...], preferred_element_type=jnp.float32)
     for block in range(blocks):
-        rows = total[block * VS_DEV : (block + 1) * VS_DEV, :].astype(jnp.bfloat16)
+        at = slice(block * VS_DEV, (block + 1) * VS_DEV)
+        real = total[at, :LANES]
+        imag = total[sources + block * VS_DEV : sources + (block + 1) * VS_DEV, LANES:]
         for group in range(groups):
-            out_ref[block * groups + group] = rows
-
-
-def pairs(got, groups):
-    blocks = got.shape[0]
+            cosine, sine = lead_ref[group : group + 1, :], lead_ref[groups + group : groups + group + 1, :]
+            out_ref[block * groups + group] = jnp.concatenate(
+                [real * cosine - imag * sine, real * sine + imag * cosine], axis=1
+            ).astype(jnp.bfloat16)
+
+
+def pairs(got, lead):
+    blocks, groups = got.shape[0], lead.shape[0] // 2
+    block_rows = (STEPS // 2 + 1) * STA * STA
     return pl.pallas_call(
         pair_kernel,
         out_shape=pltpu.VMEM((blocks * groups, VS_DEV, 2 * LANES), jnp.bfloat16),
-        in_specs=[VMEM],
+        in_specs=[VMEM] * 2,
         out_specs=VMEM,
         compiler_params=pltpu.CompilerParams(vmem_limit_bytes=KERNEL_VMEM),
         scratch_shapes=[
             pltpu.VMEM((blocks, 2 * WIN, STA, LANES), jnp.float32),
-            pltpu.VMEM((STEPS * STA * STA, 2 * LANES), jnp.bfloat16),
-            pltpu.VMEM((blocks * VS_DEV, 2 * LANES), jnp.float32),
+            pltpu.VMEM((blocks * block_rows, 2 * LANES), jnp.bfloat16),
+            pltpu.VMEM((2 * blocks * VS_DEV, blocks * block_rows), jnp.bfloat16),
+            pltpu.VMEM((2 * blocks * VS_DEV, 2 * LANES), jnp.float32),
         ],
-    )(got)
-
-
-def lag_kernel(bins_ref, wave_ref, turn_ref, out_ref, lags):
+    )(got, lead)
+
+
+def lag_kernel(bins_ref, wave_ref, turn_ref, out_ref):
     chunks = bins_ref.shape[0]
-    half = out_ref.shape[1]
     rows = bins_ref[...].reshape(chunks * VS_DEV, 2 * LANES)
-    for column in range(0, 2 * half, 256):
-        part = slice(column, column + 256)
-        lags[:, part] = jnp.dot(rows, wave_ref[0, :, part], preferred_element_type=jnp.float32) + jnp.dot(
-            rows, wave_ref[1, :, part], preferred_element_type=jnp.float32
+    for tile in range(wave_ref.shape[1]):
+        lags = jnp.dot(rows, wave_ref[0, tile], preferred_element_type=jnp.float32) + jnp.dot(
+            rows, wave_ref[1, tile], preferred_element_type=jnp.float32
         )
-    out_ref[...] = jnp.zeros_like(out_ref)
-
-    def add(chunk, carry):
-        at = pl.ds(pl.multiple_of(chunk * VS_DEV, VS_DEV), VS_DEV)
-        cosine, sine = turn_ref[0, pl.ds(chunk, 1), :], turn_ref[1, pl.ds(chunk, 1), :]
-        out_ref[...] += lags[at, :half] * cosine - lags[at, half:] * sine
-        return carry
-
-    lax.fori_loop(0, chunks, add, 0)
+        total = jnp.zeros((VS_DEV, LANES), jnp.float32)
+        for chunk in range(chunks):
+            piece = lags[chunk * VS_DEV : (chunk + 1) * VS_DEV]
+            total += piece[:, :LANES] * turn_ref[0, chunk : chunk + 1, :]
+            total -= piece[:, LANES:] * turn_ref[1, chunk : chunk + 1, :]
+        out_ref[:, tile * LANES : (tile + 1) * LANES] = total
 
 
 def lags_of(bins, wave, turn):
-    half = wave.shape[2] // 2
     return pl.pallas_call(
         lag_kernel,
-        out_shape=jax.ShapeDtypeStruct((VS_DEV, half), jnp.float32),
+        out_shape=jax.ShapeDtypeStruct((VS_DEV, wave.shape[1] * LANES), jnp.float32),
         in_specs=[VMEM] * 3,
         out_specs=VMEM,
         compiler_params=pltpu.CompilerParams(vmem_limit_bytes=KERNEL_VMEM),
-        scratch_shapes=[pltpu.VMEM((bins.shape[0] * VS_DEV, 2 * half), jnp.float32)],
     )(bins, wave, turn)
 
 
-def wave_table(first_lag, lag_dev):
-    bins = jnp.arange(LANES, dtype=jnp.int32)
-    shifts = first_lag + jnp.arange(lag_dev, dtype=jnp.int32)
-    phase = jnp.mod(bins[:, None] * shifts[None, :], 2 * BINS)
-    angle = phase.astype(jnp.float32) * (math.pi / BINS)
-    cosine, sine = jnp.cos(angle) / math.sqrt(BINS), jnp.sin(angle) / math.sqrt(BINS)
-    full = jnp.concatenate(
-        [jnp.concatenate([cosine, sine], axis=1), jnp.concatenate([-sine, cosine], axis=1)], axis=0
-    )
-    high = full.astype(jnp.bfloat16)
-    low = (full - high.astype(jnp.float32)).astype(jnp.bfloat16)
-    return jnp.stack([high, low])
-
-
-def turn_table(first_lag, lag_dev, blocks, groups):
-    places = jnp.arange(blocks * groups, dtype=jnp.int32)
-    chunk = places % groups * blocks + places // groups
-    shifts = first_lag + jnp.arange(lag_dev, dtype=jnp.int32)
-    phase = jnp.mod(LANES * chunk[:, None] * shifts[None, :], 2 * BINS)
-    angle = phase.astype(jnp.float32) * (math.pi / BINS)
-    return jnp.stack([jnp.cos(angle), jnp.sin(angle)])
+def turns(phase):
+    angle = np.mod(phase, 2 * BINS) * (math.pi / BINS)
+    return np.cos(angle), np.sin(angle)
+
+
+def lag_tables(blocks, groups):
+    lag_dev = LAGS // groups
+    first = np.arange(groups) * lag_dev - LAGS // 2
+    bins = np.arange(LANES)
+    lead = np.concatenate(turns(first[:, None] * bins[None, :])).astype(np.float32)
+    cosine, sine = turns(bins[:, None] * np.arange(lag_dev)[None, :])
+    tiles = []
+    for at in range(0, lag_dev, LANES):
+        part = slice(at, at + LANES)
+        tiles.append(np.block([[cosine[:, part], sine[:, part]], [-sine[:, part], cosine[:, part]]]))
+    wave = np.stack(tiles) / math.sqrt(BINS)
+    high = wave.astype(jnp.bfloat16)
+    low = (wave - high.astype(np.float64)).astype(jnp.bfloat16)
+    place = np.arange(blocks * groups)
+    chunk = place % groups * blocks + place // groups
+    turn = np.stack(turns(LANES * chunk[:, None] * bins[None, :])).astype(np.float32)
+    return jnp.asarray(lead), jnp.asarray(np.stack([high, low])), jnp.asarray(turn)
 
 
 def by_bins(spectra, quality, pair_mask, owners, local_rows):
     blocks, groups = lax.axis_size("blk"), lax.axis_size("grp")
-    lag_dev = LAGS // groups
-    first_lag = lax.axis_index("grp") * lag_dev - LAGS // 2
-    wave = wave_table(first_lag, lag_dev)
-    turn = turn_table(first_lag, lag_dev, blocks, groups)
+    lead, wave, turn = lag_tables(blocks, groups)
     sent = pack(spectra, quality, pair_mask, owners, local_rows, blocks)
     got = lax.all_to_all(sent, "blk", split_axis=0, concat_axis=0, tiled=True)
-    got, wave, turn = lax.optimization_barrier((got, wave, turn))
-    summed = pairs(got, groups)
+    summed = pairs(got, lead)
     bins = lax.all_to_all(summed, ("blk", "grp"), split_axis=0, concat_axis=0, tiled=True)
     return lags_of(bins, wave, turn)
 
@@ -340,7 +367,9 @@
 
 
 def on_device(spectra, quality, pair_mask, owners, local_rows):
-    if spectra.shape[3] == lax.axis_size("blk") * LANES:
+    blocks, groups = lax.axis_size("blk"), lax.axis_size("grp")
+    whole_tiles = spectra.shape[3] == blocks * LANES and LANES * (LAGS // groups) % (2 * BINS) == 0
+    if whole_tiles and blocks == STEPS + 2:
         return by_bins(spectra, quality, pair_mask, owners, local_rows)
     return by_halo(spectra, quality, pair_mask, owners, local_rows)
 

time: 32.7 us -> 30 us (0.917)
  blocking collectives: 14 us -> 24.8 us
  starting transfers between devices: 5.18 us -> 0 us
  waiting for transfers between devices: 4.04 us -> 0 us
  Pallas kernels: 7.43 us -> 4.92 us
  other arithmetic: 1.78 us -> 0 us
    all_to_all x0 -> x1, blocking collectives: none -> 10.9 us  [by_bins(): got = lax.all_to_all(sent, 'blk', split_axis=0, concat_axis=0, tiled=True)]
    all_to_all x1 -> x0, starting transfers between devices: 5.18 us -> none  [by_bins(): got = lax.all_to_all(sent, 'blk', split_axis=0, concat_axis=0, tiled=True)]
    all_to_all x1 -> x0, waiting for transfers between devices: 4.04 us -> none  [by_bins(): got = lax.all_to_all(sent, 'blk', split_axis=0, concat_axis=0, tiled=True)]
    pallas_call x1, Pallas kernels: 3.91 us -> 2.33 us  [pairs(): pl.pallas_call(pair_kernel, out_shape=pltpu.VMEM((blocks * groups, VS_DEV...]
    div x1 -> x0, other arithmetic: 1.06 us -> none  [wave_table(): jnp.sin(angle) / math.sqrt(BINS)]
    pallas_call x1, Pallas kernels: 1.75 us -> 1.26 us  [pack(): pl.pallas_call(pack_kernel, out_shape=pltpu.VMEM((blocks, SPEC_ROWS + MET...]
    pallas_call x1, Pallas kernels: 1.78 us -> 1.34 us  [lags_of(): pl.pallas_call(lag_kernel, out_shape=jax.ShapeDtypeStruct((VS_DEV, wave.s...]
    cos x1 -> x0, other arithmetic: 0.34 us -> none  [turn_table(): return jnp.stack([jnp.cos(angle), jnp.sin(angle)])]
  transfers between devices with their start and end apart: 1 -> 0, of which waited for: 1 -> 0; matrix products, arithmetic and copies ran while one was open for 5% -> 0% of each run, Pallas kernels for 0% -> 0%
where the time goes in v3:
time: 30 us; the launch traced here: 29.8 us
  blocking collectives  24.8 us (83%)
  Pallas kernels  4.92 us (16%)
    all_to_all x1, blocking collectives, by_bins(): lax.all_to_all(summed, ('blk', 'grp'), split_axis=0, concat_axis=0, tiled...  14 us
    all_to_all x1, blocking collectives, by_bins(): got = lax.all_to_all(sent, 'blk', split_axis=0, concat_axis=0, tiled=True)  10.9 us
    pallas_call x1, Pallas kernels, pairs(): pl.pallas_call(pair_kernel, out_shape=pltpu.VMEM((blocks * groups, VS_DEV...  2.33 us
    pallas_call x1, Pallas kernels, lags_of(): pl.pallas_call(lag_kernel, out_shape=jax.ShapeDtypeStruct((VS_DEV, wave.s...  1.34 us
    pallas_call x1, Pallas kernels, pack(): pl.pallas_call(pack_kernel, out_shape=pltpu.VMEM((blocks, SPEC_ROWS + MET...  1.26 us

profile of v3, /device:TPU:0, one launch (start us, length us, event | category | flops | bytes accessed | tf_op | source)
XLA Modules:
  0.0 29.8 jit_solution(2915628674182664471)
XLA Ops:
  0.0 0.0 copy-start.2
  0.0 0.0 copy-start
  0.0 1.3 %shard_map.82 = bf16[8,80,128]{2,1,0:T(8,128)(2,1)S(1)} custom-call(bf16[2,8,4,1024]{3,2,1,0:T(4,128)(2,1)} %spec_hbm.1, s32[4,8]{1,0:T(4,128)} %bitcast.5, s32[2,2,6]{2,1,0:T(2,128)} %bitcast.6, s32[1,384]{1,0:T(1,128)} %bitcast.7, s32[384]{0:T(512)} %local_hbm.1), custom_call_target="tpu_custom_call" | custom-call | tf_op jit(solution)/shard_map/pallas_call | solution.py:116
  1.3 10.9 %all_to_all.10.got_ref = bf16[8,80,128]{2,1,0:T(8,128)(2,1)S(1)} all-to-all(bf16[8,80,128]{2,1,0:T(8,128)(2,1)S(1)} %shard_map.82), channel_id=1, replica_groups=mesh['blk'=8,'grp'=4] {'blk'}, dimensions={0} | all-to-all | bytes 327680 | tf_op jit(solution)/shard_map/all_to_all | solution.py:281
  12.1 0.0 copy-done.2
  12.1 2.3 %shard_map.83 = bf16[32,16,256]{2,1,0:T(8,128)(2,1)S(1)} custom-call(bf16[8,80,128]{2,1,0:T(8,128)(2,1)S(1)} %all_to_all.10.got_ref, f32[8,128]{1,0:T(8,128)S(1)} %copy-done.2), custom_call_target="tpu_custom_call" | custom-call | tf_op jit(solution)/shard_map/pallas_call | solution.py:213
  14.5 0.0 copy-start.1
  14.5 14.0 %all_to_all.11.bins_ref = bf16[32,16,256]{2,1,0:T(8,128)(2,1)S(1)} all-to-all(bf16[32,16,256]{2,1,0:T(8,128)(2,1)S(1)} %shard_map.83), channel_id=1, replica_groups=mesh['blk'=8,'grp'=4] {'blk','grp'}, dimensions={0} | all-to-all | bytes 524288 | tf_op jit(solution)/shard_map/all_to_all | solution.py:283
  28.4 0.0 copy-done
  28.4 0.0 copy-done.1
  28.5 1.3 %shard_map.84 = f32[16,512]{1,0:T(8,128)} custom-call(bf16[32,16,256]{2,1,0:T(8,128)(2,1)S(1)} %all_to_all.11.bins_ref, bf16[2,4,256,256]{3,2,1,0:T(8,128)(2,1)S(1)} %copy-done, f32[2,32,128]{2,1,0:T(8,128)S(1)} %copy-done.1), custom_call_target="tpu_custom_call" | custom-call | tf_op jit(solution)/shard_map/pallas_call | solution.py:244
Async XLA Ops:
  0.0 12.1 %copy-start.2 = (f32[8,128]{1,0:T(8,128)S(1)}, f32[8,128]{1,0:T(8,128)}, u32[]{:S(2)}) copy-start(f32[8,128]{1,0:T(8,128)} %constant.6.clone.lead_ref) | copy-start | bytes 12292
  0.0 28.4 %copy-start = (bf16[2,4,256,256]{3,2,1,0:T(8,128)(2,1)S(1)}, bf16[2,4,256,256]{3,2,1,0:T(8,128)(2,1)}, u32[]{:S(2)}) copy-start(bf16[2,4,256,256]{3,2,1,0:T(8,128)(2,1)} %constant.7.clone.wave_ref) | copy-start | bytes 3145732
  14.5 14.0 %copy-start.1 = (f32[2,32,128]{2,1,0:T(8,128)S(1)}, f32[2,32,128]{2,1,0:T(8,128)}, u32[]{:S(2)}) copy-start(f32[2,32,128]{2,1,0:T(8,128)} %constant.8.clone.turn_ref) | copy-start | bytes 98308

commit v4 on v3

--- a/solution.py
+++ b/solution.py
@@ -17,57 +17,33 @@
 SUB = 4
 VS_DEV = 16
 LANES = 128
-SPEC_ROWS = 2 * WIN * STA
-META_ROWS = 16
+SPEC_TILES = 2 * STA
 KERNEL_VMEM = 12 * 1024 * 1024
 
 VMEM = pl.BlockSpec(memory_space=pltpu.VMEM)
 
 
-def pack_kernel(
-    spec_hbm,
-    weight_hbm,
-    mask_hbm,
-    owner_hbm,
-    local_hbm,
-    out_ref,
-    spec_ref,
-    weight_ref,
-    mask_ref,
-    owner_ref,
-    local_ref,
-    plain,
-    arrived,
-):
+def pack_kernel(spec_hbm, weight_hbm, mask_hbm, owner_hbm, local_hbm, out_ref, weight_ref, mask_ref, owner_ref, local_ref, sliced, arrived):
     dests = out_ref.shape[0]
+    slices = [
+        pltpu.make_async_copy(
+            spec_hbm.at[:, :, pl.ds(dest * LANES, LANES)],
+            out_ref.at[dest, pl.ds(0, SPEC_TILES)],
+            sliced.at[dest],
+        )
+        for dest in range(dests)
+    ]
+    small = [(weight_hbm, weight_ref), (mask_hbm, mask_ref), (owner_hbm, owner_ref), (local_hbm, local_ref)]
     moves = [
         pltpu.make_async_copy(source, target, arrived.at[place])
-        for place, (source, target) in enumerate(
-            [
-                (spec_hbm, spec_ref),
-                (weight_hbm, weight_ref),
-                (mask_hbm, mask_ref),
-                (owner_hbm, owner_ref),
-                (local_hbm, local_ref),
-            ]
-        )
+        for place, (source, target) in enumerate(small)
     ]
-    for move in moves:
+    for move in moves + slices:
         move.start()
     lane = lax.broadcasted_iota(jnp.int32, (1, LANES), 1)
-    lane_in = lax.broadcasted_iota(jnp.int32, (LANES, LANES), 0)
-    lane_out = lax.broadcasted_iota(jnp.int32, (LANES, LANES), 1)
-    turned = lane_out // 64 * 64 + lane_out % STA * STA + lane_out % 64 // STA
-    swap = (lane_in == turned).astype(jnp.float32).astype(jnp.bfloat16)
     for move in moves:
         move.wait()
-    for part in range(2):
-        for station in range(STA):
-            first = part * STA * WIN + station * WIN
-            values = spec_ref[part, station].astype(jnp.float32)
-            for dest in range(dests):
-                plain[dest, first : first + WIN, :] = values[:, dest * LANES : (dest + 1) * LANES]
-    labels = []
+    rows = []
     for chunk in range(STEPS // 2):
         part = slice(chunk * LANES, (chunk + 1) * LANES)
         mask = jnp.zeros((1, LANES), jnp.int32)
@@ -78,36 +54,20 @@
                     step = chunk * 2 + odd
                     mask = jnp.where(here, mask_ref[near, far : far + 1, step : step + 1], mask)
         source = owner_ref[:, part] * VS_DEV + local_ref[part].reshape(1, LANES)
-        labels.append(jnp.where(mask != 0, source, -1).astype(jnp.float32))
-    last = jnp.broadcast_to(labels[2], (STA, LANES)).astype(jnp.bfloat16)
-    labels[2] = jnp.dot(last, swap, preferred_element_type=jnp.float32)[:1]
-    station_of = lax.broadcasted_iota(jnp.int32, (STA, STA), 0)
-    on_lane = lax.broadcasted_iota(jnp.int32, (STA, STA), 1)
-    wide = lax.broadcasted_iota(jnp.int32, (STA, LANES), 1)
-    weights = jnp.zeros((STA, LANES), jnp.float32)
-    for window in range(WIN):
-        row = weight_ref[window : window + 1, :].astype(jnp.float32)
-        column = jnp.sum(jnp.where(station_of == on_lane, row, 0.0), axis=1, keepdims=True)
-        weights = jnp.where(wide == window, column, weights)
-    meta = jnp.concatenate(labels + [jnp.zeros((5, LANES), jnp.float32), weights], axis=0).astype(jnp.bfloat16)
+        rows.append(jnp.where(mask != 0, source, -1).astype(jnp.float32))
+    weights = [weight_ref[window : window + 1, :].astype(jnp.float32) for window in range(WIN)]
+    rows.append(jnp.concatenate(weights + [jnp.zeros((1, LANES - WIN * STA), jnp.float32)], axis=1))
+    meta = jnp.concatenate(rows, axis=0).astype(jnp.bfloat16)
     for dest in range(dests):
-        for part in range(2):
-            for window in range(0, WIN, 2):
-                pair = [
-                    plain[dest, pl.ds(part * STA * WIN + window + more, STA, stride=WIN), :]
-                    for more in range(2)
-                ]
-                first = part * STA * WIN + window * STA
-                out_ref[dest, first : first + 2 * STA, :] = jnp.concatenate(pair, axis=0).astype(
-                    jnp.bfloat16
-                )
-        out_ref[dest, SPEC_ROWS:, :] = meta
+        out_ref[dest, SPEC_TILES] = meta
+    for move in slices:
+        move.wait()
 
 
 def pack(spectra, quality, pair_mask, owners, local_rows, blocks):
     rows = owners.shape[0]
     operands = (
-        spectra,
+        spectra.reshape(SPEC_TILES, WIN, spectra.shape[3]),
         quality.T,
         pair_mask[0].transpose(1, 2, 0),
         owners.reshape(1, rows),
@@ -115,91 +75,95 @@
     )
     return pl.pallas_call(
         pack_kernel,
-        out_shape=pltpu.VMEM((blocks, SPEC_ROWS + META_ROWS, LANES), jnp.bfloat16),
+        out_shape=pltpu.VMEM((blocks, SPEC_TILES + 1, WIN, LANES), jnp.bfloat16),
         in_specs=[pl.BlockSpec(memory_space=pltpu.HBM)] * len(operands),
         out_specs=VMEM,
         compiler_params=pltpu.CompilerParams(vmem_limit_bytes=KERNEL_VMEM),
-        scratch_shapes=[pltpu.VMEM(each.shape, each.dtype) for each in operands]
-        + [
-            pltpu.VMEM((blocks, SPEC_ROWS, LANES), jnp.float32),
-            pltpu.SemaphoreType.DMA((len(operands),)),
-        ],
+        scratch_shapes=[pltpu.VMEM(each.shape, each.dtype) for each in operands[1:]]
+        + [pltpu.SemaphoreType.DMA((blocks,)), pltpu.SemaphoreType.DMA((len(operands) - 1,))],
     )(*[pltpu.with_memory_space_constraint(each, pltpu.HBM) for each in operands])
 
 
-def pair_kernel(got_ref, lead_ref, out_ref, spec, phat, hot, total):
+def pair_kernel(got_ref, lead_hbm, out_ref, lead_ref, plain, meta, own_spec, far_spec, names, phat, hot, total, arrived):
     blocks = got_ref.shape[0]
     groups = out_ref.shape[0] // blocks
     sources = blocks * VS_DEV
-    kept = STEPS // 2 + 1
-    block_rows = kept * STA * STA
-
-    for block in range(blocks):
-        weights = got_ref[block, SPEC_ROWS : SPEC_ROWS + META_ROWS, :].astype(jnp.float32)[STA:]
-        columns = [weights[:, window : window + 1] for window in range(WIN)]
-        for first in range(0, SPEC_ROWS, 2 * STA):
-            both = got_ref[block, first : first + 2 * STA, :].astype(jnp.float32)
-            for more in range(2):
-                place = first // STA + more
-                spec[block, place] = both[more * STA : (more + 1) * STA] * columns[place % WIN]
-
+    tile_rows = STA * STA
+    lead_move = pltpu.make_async_copy(lead_hbm, lead_ref, arrived)
+    lead_move.start()
+
+    for block in range(blocks):
+        for tile in range(SPEC_TILES):
+            plain[block, tile * WIN : (tile + 1) * WIN, :] = got_ref[block, tile].astype(jnp.float32)
+        meta[block * WIN : (block + 1) * WIN, :] = got_ref[block, SPEC_TILES].astype(jnp.float32)
+    weights = meta[pl.ds(WIN - 1, blocks, stride=WIN), :].T
+    for block in range(blocks):
+        for window in range(WIN):
+            column = weights[window * STA : (window + 1) * STA, block : block + 1]
+            real = plain[block, pl.ds(window, STA, stride=WIN), :] * column
+            imag = plain[block, pl.ds(STA * WIN + window, STA, stride=WIN), :] * column
+            for place, (near, far) in enumerate([(real, real), (imag, imag), (real + imag, real - imag)]):
+                own_spec[block, place * WIN + window] = near
+                far_spec[block, place * WIN + window] = far
+
+    lane_in = lax.broadcasted_iota(jnp.int32, (LANES, LANES), 0)
+    lane_out = lax.broadcasted_iota(jnp.int32, (LANES, LANES), 1)
+    turned = lane_out // tile_rows * tile_rows + lane_out % STA * STA + lane_out % tile_rows // STA
+    swap = (lane_in == turned).astype(jnp.float32).astype(jnp.bfloat16)
+    for chunk in range(STEPS // 2):
+        here = meta[pl.ds(chunk, blocks, stride=WIN), :]
+        if chunk:
+            other = jnp.dot(here.astype(jnp.bfloat16), swap, preferred_element_type=jnp.float32)
+            if chunk == 1:
+                block_of = lax.broadcasted_iota(jnp.int32, here.shape, 0)
+                lane = lax.broadcasted_iota(jnp.int32, here.shape, 1)
+                other = jnp.where((block_of >= blocks // 2) & (lane >= tile_rows), other, here)
+            here = other
+        names[chunk] = here
     source = lax.broadcasted_iota(jnp.int32, (sources, LANES), 0).astype(jnp.float32)
-    lane = lax.broadcasted_iota(jnp.int32, (1, LANES), 1)
-
-    def earlier(block, by):
-        return lax.rem(block - by + blocks, blocks)
-
-    def names(block, chunk):
-        rows = got_ref[block, SPEC_ROWS : SPEC_ROWS + META_ROWS, :].astype(jnp.float32)
-        return rows[chunk : chunk + 1]
-
-    def correlate(block, carry):
-        base = pl.multiple_of(block * block_rows, block_rows)
+    for block in range(blocks):
+        for chunk in range(STEPS // 2):
+            at = (block * STEPS + 2 * chunk) * tile_rows
+            label = names[chunk, block : block + 1, :]
+            hot[:, at : at + LANES] = (source == label).astype(jnp.float32).astype(jnp.bfloat16)
+
+    for block in range(blocks):
+        steps = STEPS // 2 + (block < blocks // 2)
         for near in range(0, STA, 2):
             own = [
                 [
-                    jnp.broadcast_to(spec[block, place, near + more : near + more + 1, :], (STA, LANES))
-                    for place in range(2 * WIN)
+                    jnp.broadcast_to(own_spec[block, place, near + more : near + more + 1, :], (STA, LANES))
+                    for place in range(3 * WIN)
                 ]
                 for more in range(2)
             ]
-            for step in range(kept):
-                far_block = earlier(block, 1 + step)
-                far = [spec[far_block, place] for place in range(2 * WIN)]
+            for step in range(steps):
+                far_block = (block - 1 - step) % blocks
+                far = [far_spec[far_block, place] for place in range(3 * WIN)]
                 rows = []
                 for more in range(2):
-                    real, imag = 0.0, 0.0
-                    for window in range(WIN):
-                        a_real, a_imag = own[more][window], own[more][WIN + window]
-                        b_real, b_imag = far[window], far[WIN + window]
-                        real += a_real * b_real + a_imag * b_imag
-                        imag += a_imag * b_real - a_real * b_imag
+                    sums = [
+                        sum(own[more][place] * far[place] for place in range(kind * WIN, (kind + 1) * WIN))
+                        for kind in range(3)
+                    ]
+                    real, imag = sums[0] + sums[1], sums[2] - sums[0] + sums[1]
                     factor = lax.rsqrt(jnp.maximum(real * real + imag * imag, 1.0))
                     rows.append((real * factor, imag * factor))
-                at = base + (step * STA * STA + near * STA)
-                for part in range(2):
-                    tile = jnp.concatenate([rows[0][part], rows[1][part]], axis=0)
-                    phat[pl.ds(pl.multiple_of(at, 2 * STA), 2 * STA), part * LANES : (part + 1) * LANES] = (
-                        tile.astype(jnp.bfloat16)
-                    )
-        again = [
-            jnp.where(lane >= LANES // 2, names(earlier(block, 2), 2), -1.0),
-            jnp.where(lane < LANES // 2, names(earlier(block, 3), 2), -1.0),
-        ]
-        for chunk in range(2):
-            forth = (source == names(block, chunk)).astype(jnp.float32)
-            back = (source == again[chunk]).astype(jnp.float32)
-            at = pl.ds(pl.multiple_of(base + chunk * LANES, LANES), LANES)
-            hot[:sources, at] = (forth + back).astype(jnp.bfloat16)
-            hot[sources:, at] = (forth - back).astype(jnp.bfloat16)
-        return carry
-
-    lax.fori_loop(0, blocks, correlate, 0)
+                real = jnp.concatenate([rows[0][0], rows[1][0]], axis=0).astype(jnp.bfloat16)
+                imag = jnp.concatenate([rows[0][1], rows[1][1]], axis=0).astype(jnp.bfloat16)
+                at = (block * STEPS + step) * tile_rows + near * STA
+                phat[at : at + 2 * STA, :LANES] = real
+                phat[at : at + 2 * STA, LANES:] = imag
+                back = blocks - 2 - step
+                if back < STEPS:
+                    at = (far_block * STEPS + back) * tile_rows + near * STA
+                    phat[at : at + 2 * STA, :LANES] = real
+                    phat[at : at + 2 * STA, LANES:] = -imag
     total[...] = jnp.dot(hot[...], phat[...], preferred_element_type=jnp.float32)
+    lead_move.wait()
     for block in range(blocks):
         at = slice(block * VS_DEV, (block + 1) * VS_DEV)
-        real = total[at, :LANES]
-        imag = total[sources + block * VS_DEV : sources + (block + 1) * VS_DEV, LANES:]
+        real, imag = total[at, :LANES], total[at, LANES:]
         for group in range(groups):
             cosine, sine = lead_ref[group : group + 1, :], lead_ref[groups + group : groups + group + 1, :]
             out_ref[block * groups + group] = jnp.concatenate(
@@ -209,20 +173,26 @@
 
 def pairs(got, lead):
     blocks, groups = got.shape[0], lead.shape[0] // 2
-    block_rows = (STEPS // 2 + 1) * STA * STA
+    sources, rows = blocks * VS_DEV, blocks * STEPS * STA * STA
     return pl.pallas_call(
         pair_kernel,
         out_shape=pltpu.VMEM((blocks * groups, VS_DEV, 2 * LANES), jnp.bfloat16),
-        in_specs=[VMEM] * 2,
+        in_specs=[VMEM, pl.BlockSpec(memory_space=pltpu.HBM)],
         out_specs=VMEM,
         compiler_params=pltpu.CompilerParams(vmem_limit_bytes=KERNEL_VMEM),
         scratch_shapes=[
-            pltpu.VMEM((blocks, 2 * WIN, STA, LANES), jnp.float32),
-            pltpu.VMEM((blocks * block_rows, 2 * LANES), jnp.bfloat16),
-            pltpu.VMEM((2 * blocks * VS_DEV, blocks * block_rows), jnp.bfloat16),
-            pltpu.VMEM((2 * blocks * VS_DEV, 2 * LANES), jnp.float32),
+            pltpu.VMEM(lead.shape, lead.dtype),
+            pltpu.VMEM((blocks, SPEC_TILES * WIN, LANES), jnp.float32),
+            pltpu.VMEM((blocks * WIN, LANES), jnp.float32),
+            pltpu.VMEM((blocks, 3 * WIN, STA, LANES), jnp.float32),
+            pltpu.VMEM((blocks, 3 * WIN, STA, LANES), jnp.float32),
+            pltpu.VMEM((STEPS // 2, blocks, LANES), jnp.float32),
+            pltpu.VMEM((rows, 2 * LANES), jnp.bfloat16),
+            pltpu.VMEM((sources, rows), jnp.bfloat16),
+            pltpu.VMEM((sources, 2 * LANES), jnp.float32),
+            pltpu.SemaphoreType.DMA,
         ],
-    )(got, lead)
+    )(got, pltpu.with_memory_space_constraint(lead, pltpu.HBM))
 
 
 def lag_kernel(bins_ref, wave_ref, turn_ref, out_ref):

time: 30 us -> 29.1 us (0.970)
  Pallas kernels: 4.92 us -> 4.26 us
    pallas_call x1, Pallas kernels: 2.33 us -> 1.8 us  [pairs(): pl.pallas_call(pair_kernel, out_shape=pltpu.VMEM((blocks * groups, VS_DEV...]
where the time goes in v4:
time: 29.1 us; the launch traced here: 28.9 us
  blocking collectives  24.6 us (85%)
  Pallas kernels  4.26 us (15%)
    all_to_all x1, blocking collectives, by_bins(): lax.all_to_all(summed, ('blk', 'grp'), split_axis=0, concat_axis=0, tiled...  14 us
    all_to_all x1, blocking collectives, by_bins(): got = lax.all_to_all(sent, 'blk', split_axis=0, concat_axis=0, tiled=True)  10.6 us
    pallas_call x1, Pallas kernels, pairs(): pl.pallas_call(pair_kernel, out_shape=pltpu.VMEM((blocks * groups, VS_DEV...  1.8 us
    pallas_call x1, Pallas kernels, lags_of(): pl.pallas_call(lag_kernel, out_shape=jax.ShapeDtypeStruct((VS_DEV, wave.s...  1.34 us
    pallas_call x1, Pallas kernels, pack(): pl.pallas_call(pack_kernel, out_shape=pltpu.VMEM((blocks, SPEC_TILES + 1,...  1.13 us

profile of v4, /device:TPU:0, one launch (start us, length us, event | category | flops | bytes accessed | tf_op | source)
XLA Modules:
  0.0 28.9 jit_solution(769347192364211650)
XLA Ops:
  0.0 0.0 copy-start
  0.0 1.1 %shard_map.82 = bf16[8,17,4,128]{3,2,1,0:T(4,128)(2,1)S(1)} custom-call(bf16[16,4,1024]{2,1,0:T(4,128)(2,1)} %bitcast.6, s32[4,8]{1,0:T(4,128)} %bitcast.7, s32[2,2,6]{2,1,0:T(2,128)} %bitcast.8, s32[1,384]{1,0:T(1,128)} %bitcast.9, s32[384]{0:T(512)} %local_hbm.1), custom_call_target="tpu_custom_call" | custom-call | tf_op jit(solution)/shard_map/pallas_call | solution.py:76
  1.1 10.6 %all_to_all.10.got_ref = bf16[8,17,4,128]{3,2,1,0:T(4,128)(2,1)S(1)} all-to-all(bf16[8,17,4,128]{3,2,1,0:T(4,128)(2,1)S(1)} %shard_map.82), channel_id=1, replica_groups=mesh['blk'=8,'grp'=4] {'blk'}, dimensions={0} | all-to-all | bytes 278528 | tf_op jit(solution)/shard_map/all_to_all | solution.py:251
  11.7 1.8 %shard_map.83 = bf16[32,16,256]{2,1,0:T(8,128)(2,1)S(1)} custom-call(bf16[8,17,4,128]{3,2,1,0:T(4,128)(2,1)S(1)} %all_to_all.10.got_ref, f32[8,128]{1,0:T(8,128)} %constant.6.clone.lead_hbm), custom_call_target="tpu_custom_call" | custom-call | tf_op jit(solution)/shard_map/pallas_call | solution.py:177
  13.5 0.0 copy-start.1
  13.5 14.0 %all_to_all.11.bins_ref = bf16[32,16,256]{2,1,0:T(8,128)(2,1)S(1)} all-to-all(bf16[32,16,256]{2,1,0:T(8,128)(2,1)S(1)} %shard_map.83), channel_id=1, replica_groups=mesh['blk'=8,'grp'=4] {'blk','grp'}, dimensions={0} | all-to-all | bytes 524288 | tf_op jit(solution)/shard_map/all_to_all | solution.py:253
  27.5 0.0 copy-done
  27.5 0.0 copy-done.1
  27.5 1.3 %shard_map.84 = f32[16,512]{1,0:T(8,128)} custom-call(bf16[32,16,256]{2,1,0:T(8,128)(2,1)S(1)} %all_to_all.11.bins_ref, bf16[2,4,256,256]{3,2,1,0:T(8,128)(2,1)S(1)} %copy-done, f32[2,32,128]{2,1,0:T(8,128)S(1)} %copy-done.1), custom_call_target="tpu_custom_call" | custom-call | tf_op jit(solution)/shard_map/pallas_call | solution.py:214
Async XLA Ops:
  0.0 27.5 %copy-start = (bf16[2,4,256,256]{3,2,1,0:T(8,128)(2,1)S(1)}, bf16[2,4,256,256]{3,2,1,0:T(8,128)(2,1)}, u32[]{:S(2)}) copy-start(bf16[2,4,256,256]{3,2,1,0:T(8,128)(2,1)} %constant.7.clone.wave_ref) | copy-start | bytes 3145732
  13.5 14.0 %copy-start.1 = (f32[2,32,128]{2,1,0:T(8,128)S(1)}, f32[2,32,128]{2,1,0:T(8,128)}, u32[]{:S(2)}) copy-start(f32[2,32,128]{2,1,0:T(8,128)} %constant.8.clone.turn_ref) | copy-start | bytes 98308

commit v5 on v4

--- a/solution.py
+++ b/solution.py
@@ -89,17 +89,21 @@
     groups = out_ref.shape[0] // blocks
     sources = blocks * VS_DEV
     tile_rows = STA * STA
-    lead_move = pltpu.make_async_copy(lead_hbm, lead_ref, arrived)
+    chunk_here = lax.axis_index("grp") * blocks + lax.axis_index("blk")
+    lead_move = pltpu.make_async_copy(lead_hbm.at[chunk_here], lead_ref, arrived)
     lead_move.start()
 
     for block in range(blocks):
         for tile in range(SPEC_TILES):
             plain[block, tile * WIN : (tile + 1) * WIN, :] = got_ref[block, tile].astype(jnp.float32)
         meta[block * WIN : (block + 1) * WIN, :] = got_ref[block, SPEC_TILES].astype(jnp.float32)
-    weights = meta[pl.ds(WIN - 1, blocks, stride=WIN), :].T
+    weights = meta[pl.ds(WIN - 1, blocks, stride=WIN), :]
+    station_of = lax.broadcasted_iota(jnp.int32, (STA, LANES), 0)
+    on_lane = lax.broadcasted_iota(jnp.int32, (STA, LANES), 1)
     for block in range(blocks):
         for window in range(WIN):
-            column = weights[window * STA : (window + 1) * STA, block : block + 1]
+            mine = jnp.where(on_lane == window * STA + station_of, weights[block : block + 1, :], 0.0)
+            column = jnp.sum(mine, axis=1, keepdims=True)
             real = plain[block, pl.ds(window, STA, stride=WIN), :] * column
             imag = plain[block, pl.ds(STA * WIN + window, STA, stride=WIN), :] * column
             for place, (near, far) in enumerate([(real, real), (imag, imag), (real + imag, real - imag)]):
@@ -172,7 +176,7 @@
 
 
 def pairs(got, lead):
-    blocks, groups = got.shape[0], lead.shape[0] // 2
+    blocks, groups = got.shape[0], lead.shape[1] // 2
     sources, rows = blocks * VS_DEV, blocks * STEPS * STA * STA
     return pl.pallas_call(
         pair_kernel,
@@ -181,7 +185,7 @@
         out_specs=VMEM,
         compiler_params=pltpu.CompilerParams(vmem_limit_bytes=KERNEL_VMEM),
         scratch_shapes=[
-            pltpu.VMEM(lead.shape, lead.dtype),
+            pltpu.VMEM(lead.shape[1:], lead.dtype),
             pltpu.VMEM((blocks, SPEC_TILES * WIN, LANES), jnp.float32),
             pltpu.VMEM((blocks * WIN, LANES), jnp.float32),
             pltpu.VMEM((blocks, 3 * WIN, STA, LANES), jnp.float32),
@@ -198,22 +202,26 @@
 def lag_kernel(bins_ref, wave_ref, turn_ref, out_ref):
     chunks = bins_ref.shape[0]
     rows = bins_ref[...].reshape(chunks * VS_DEV, 2 * LANES)
-    for tile in range(wave_ref.shape[1]):
-        lags = jnp.dot(rows, wave_ref[0, tile], preferred_element_type=jnp.float32) + jnp.dot(
-            rows, wave_ref[1, tile], preferred_element_type=jnp.float32
-        )
-        total = jnp.zeros((VS_DEV, LANES), jnp.float32)
+    twice = [jnp.concatenate([rows[:, part * LANES : (part + 1) * LANES]] * 2, axis=1) for part in range(2)]
+    tiles = wave_ref.shape[0]
+    mirror = LANES - 1 - lax.broadcasted_iota(jnp.int32, (VS_DEV, LANES), 1)
+    for tile in range(tiles):
+        real, imag = [jnp.dot(each, wave_ref[tile], preferred_element_type=jnp.float32) for each in twice]
+        even, odd = jnp.zeros((VS_DEV, LANES), jnp.float32), jnp.zeros((VS_DEV, LANES), jnp.float32)
         for chunk in range(chunks):
-            piece = lags[chunk * VS_DEV : (chunk + 1) * VS_DEV]
-            total += piece[:, :LANES] * turn_ref[0, chunk : chunk + 1, :]
-            total -= piece[:, LANES:] * turn_ref[1, chunk : chunk + 1, :]
-        out_ref[:, tile * LANES : (tile + 1) * LANES] = total
+            at = slice(chunk * VS_DEV, (chunk + 1) * VS_DEV)
+            cosine, sine = turn_ref[0, chunk : chunk + 1, :], turn_ref[1, chunk : chunk + 1, :]
+            even += real[at, :LANES] * cosine - real[at, LANES:] * sine
+            odd += imag[at, :LANES] * sine + imag[at, LANES:] * cosine
+        after, before = tiles + tile, tiles - 1 - tile
+        out_ref[:, after * LANES : (after + 1) * LANES] = even - odd
+        out_ref[:, before * LANES : (before + 1) * LANES] = jnp.take_along_axis(even + odd, mirror, axis=1)
 
 
 def lags_of(bins, wave, turn):
     return pl.pallas_call(
         lag_kernel,
-        out_shape=jax.ShapeDtypeStruct((VS_DEV, wave.shape[1] * LANES), jnp.float32),
+        out_shape=jax.ShapeDtypeStruct((VS_DEV, 2 * wave.shape[0] * LANES), jnp.float32),
         in_specs=[VMEM] * 3,
         out_specs=VMEM,
         compiler_params=pltpu.CompilerParams(vmem_limit_bytes=KERNEL_VMEM),
@@ -227,21 +235,21 @@
 
 def lag_tables(blocks, groups):
     lag_dev = LAGS // groups
-    first = np.arange(groups) * lag_dev - LAGS // 2
+    chunks = blocks * groups
+    middle = np.arange(groups) * lag_dev - LAGS // 2 + (lag_dev - 1) / 2
     bins = np.arange(LANES)
-    lead = np.concatenate(turns(first[:, None] * bins[None, :])).astype(np.float32)
-    cosine, sine = turns(bins[:, None] * np.arange(lag_dev)[None, :])
+    whole = LANES * np.arange(chunks)[:, None, None] + bins
+    lead = np.concatenate(turns(whole * middle[:, None]), axis=1).astype(np.float32)
     tiles = []
-    for at in range(0, lag_dev, LANES):
-        part = slice(at, at + LANES)
-        tiles.append(np.block([[cosine[:, part], sine[:, part]], [-sine[:, part], cosine[:, part]]]))
+    for first in range(0, lag_dev // 2, LANES):
+        tiles.append(np.concatenate(turns(bins[:, None] * (first + bins + 0.5)), axis=1))
     wave = np.stack(tiles) / math.sqrt(BINS)
     high = wave.astype(jnp.bfloat16)
     low = (wave - high.astype(np.float64)).astype(jnp.bfloat16)
-    place = np.arange(blocks * groups)
+    place = np.arange(chunks)
     chunk = place % groups * blocks + place // groups
-    turn = np.stack(turns(LANES * chunk[:, None] * bins[None, :])).astype(np.float32)
-    return jnp.asarray(lead), jnp.asarray(np.stack([high, low])), jnp.asarray(turn)
+    turn = np.stack(turns(LANES * chunk[:, None] * (bins + 0.5))).astype(np.float32)
+    return jnp.asarray(lead), jnp.asarray(np.concatenate([high, low], axis=1)), jnp.asarray(turn)
 
 
 def by_bins(spectra, quality, pair_mask, owners, local_rows):
@@ -338,7 +346,7 @@
 
 def on_device(spectra, quality, pair_mask, owners, local_rows):
     blocks, groups = lax.axis_size("blk"), lax.axis_size("grp")
-    whole_tiles = spectra.shape[3] == blocks * LANES and LANES * (LAGS // groups) % (2 * BINS) == 0
+    whole_tiles = spectra.shape[3] == blocks * LANES and LAGS // groups % (2 * LANES) == 0
     if whole_tiles and blocks == STEPS + 2:
         return by_bins(spectra, quality, pair_mask, owners, local_rows)
     return by_halo(spectra, quality, pair_mask, owners, local_rows)

time: 29.1 us -> 28.7 us (0.986)
  Pallas kernels: 4.26 us -> 3.89 us
where the time goes in v5:
time: 28.7 us; the launch traced here: 28.5 us
  blocking collectives  24.6 us (86%)
  Pallas kernels  3.89 us (14%)
    all_to_all x1, blocking collectives, by_bins(): lax.all_to_all(summed, ('blk', 'grp'), split_axis=0, concat_axis=0, tiled...  14 us
    all_to_all x1, blocking collectives, by_bins(): got = lax.all_to_all(sent, 'blk', split_axis=0, concat_axis=0, tiled=True)  10.6 us
    pallas_call x1, Pallas kernels, pairs(): pl.pallas_call(pair_kernel, out_shape=pltpu.VMEM((blocks * groups, VS_DEV...  1.71 us
    pallas_call x1, Pallas kernels, lags_of(): pl.pallas_call(lag_kernel, out_shape=jax.ShapeDtypeStruct((VS_DEV, 2 * wa...  1.13 us
    pallas_call x1, Pallas kernels, pack(): pl.pallas_call(pack_kernel, out_shape=pltpu.VMEM((blocks, SPEC_TILES + 1,...  1.05 us

profile of v5, /device:TPU:0, one launch (start us, length us, event | category | flops | bytes accessed | tf_op | source)
XLA Modules:
  0.0 28.5 jit_solution(8731480872037045030)
XLA Ops:
  0.0 1.1 %shard_map.82 = bf16[8,17,4,128]{3,2,1,0:T(4,128)(2,1)S(1)} custom-call(bf16[16,4,1024]{2,1,0:T(4,128)(2,1)} %bitcast.6, s32[4,8]{1,0:T(4,128)} %bitcast.7, s32[2,2,6]{2,1,0:T(2,128)} %bitcast.8, s32[1,384]{1,0:T(1,128)} %bitcast.9, s32[384]{0:T(512)} %local_hbm.1), custom_call_target="tpu_custom_call" | custom-call | tf_op jit(solution)/shard_map/pallas_call | solution.py:76
  1.1 10.6 %all_to_all.10.got_ref = bf16[8,17,4,128]{3,2,1,0:T(4,128)(2,1)S(1)} all-to-all(bf16[8,17,4,128]{3,2,1,0:T(4,128)(2,1)S(1)} %shard_map.82), channel_id=1, replica_groups=mesh['blk'=8,'grp'=4] {'blk'}, dimensions={0} | all-to-all | bytes 278528 | tf_op jit(solution)/shard_map/all_to_all | solution.py:259
  11.6 1.7 %shard_map.83 = bf16[32,16,256]{2,1,0:T(8,128)(2,1)S(1)} custom-call(bf16[8,17,4,128]{3,2,1,0:T(4,128)(2,1)S(1)} %all_to_all.10.got_ref, f32[32,8,128]{2,1,0:T(8,128)} %constant.6.clone.lead_hbm), custom_call_target="tpu_custom_call" | custom-call | tf_op jit(solution)/shard_map/pallas_call | solution.py:181
  13.4 0.0 copy-start
  13.4 0.0 copy-start.1
  13.4 14.0 %all_to_all.11.bins_ref = bf16[32,16,256]{2,1,0:T(8,128)(2,1)S(1)} all-to-all(bf16[32,16,256]{2,1,0:T(8,128)(2,1)S(1)} %shard_map.83), channel_id=1, replica_groups=mesh['blk'=8,'grp'=4] {'blk','grp'}, dimensions={0} | all-to-all | bytes 524288 | tf_op jit(solution)/shard_map/all_to_all | solution.py:261
  27.4 0.0 copy-done
  27.4 0.0 copy-done.1
  27.4 1.1 %shard_map.84 = f32[16,512]{1,0:T(8,128)} custom-call(bf16[32,16,256]{2,1,0:T(8,128)(2,1)S(1)} %all_to_all.11.bins_ref, bf16[2,256,256]{2,1,0:T(8,128)(2,1)S(1)} %copy-done, f32[2,32,128]{2,1,0:T(8,128)S(1)} %copy-done.1), custom_call_target="tpu_custom_call" | custom-call | tf_op jit(solution)/shard_map/pallas_call | solution.py:222
Async XLA Ops:
  13.4 14.0 %copy-start = (bf16[2,256,256]{2,1,0:T(8,128)(2,1)S(1)}, bf16[2,256,256]{2,1,0:T(8,128)(2,1)}, u32[]{:S(2)}) copy-start(bf16[2,256,256]{2,1,0:T(8,128)(2,1)} %constant.7.clone.wave_ref) | copy-start | bytes 786436
  13.4 14.0 %copy-start.1 = (f32[2,32,128]{2,1,0:T(8,128)S(1)}, f32[2,32,128]{2,1,0:T(8,128)}, u32[]{:S(2)}) copy-start(f32[2,32,128]{2,1,0:T(8,128)} %constant.8.clone.turn_ref) | copy-start | bytes 98308

commit v6 on v5

--- a/solution.py
+++ b/solution.py
@@ -18,6 +18,7 @@
 VS_DEV = 16
 LANES = 128
 SPEC_TILES = 2 * STA
+HALF_TILE = 16
 KERNEL_VMEM = 12 * 1024 * 1024
 
 VMEM = pl.BlockSpec(memory_space=pltpu.VMEM)
@@ -124,12 +125,16 @@
                 other = jnp.where((block_of >= blocks // 2) & (lane >= tile_rows), other, here)
             here = other
         names[chunk] = here
-    source = lax.broadcasted_iota(jnp.int32, (sources, LANES), 0).astype(jnp.float32)
+    source = lax.broadcasted_iota(jnp.int32, (sources, LANES), 0).astype(jnp.float32).astype(jnp.bfloat16)
+    one, zero = jnp.ones((HALF_TILE, LANES), jnp.bfloat16), jnp.zeros((HALF_TILE, LANES), jnp.bfloat16)
     for block in range(blocks):
         for chunk in range(STEPS // 2):
             at = (block * STEPS + 2 * chunk) * tile_rows
             label = names[chunk, block : block + 1, :]
-            hot[:, at : at + LANES] = (source == label).astype(jnp.float32).astype(jnp.bfloat16)
+            wanted = jnp.broadcast_to(label, (HALF_TILE, LANES)).astype(jnp.bfloat16)
+            for first in range(0, sources, HALF_TILE):
+                rows = slice(first, first + HALF_TILE)
+                hot[rows, at : at + LANES] = jnp.where(source[rows] == wanted, one, zero)
 
     for block in range(blocks):
         steps = STEPS // 2 + (block < blocks // 2)
@@ -186,8 +191,8 @@
         compiler_params=pltpu.CompilerParams(vmem_limit_bytes=KERNEL_VMEM),
         scratch_shapes=[
             pltpu.VMEM(lead.shape[1:], lead.dtype),
-            pltpu.VMEM((blocks, SPEC_TILES * WIN, LANES), jnp.float32),
-            pltpu.VMEM((blocks * WIN, LANES), jnp.float32),
+            pltpu.VMEM((blocks, SPEC_TILES * WIN + STA, LANES), jnp.float32),
+            pltpu.VMEM((blocks * WIN + STA, LANES), jnp.float32),
             pltpu.VMEM((blocks, 3 * WIN, STA, LANES), jnp.float32),
             pltpu.VMEM((blocks, 3 * WIN, STA, LANES), jnp.float32),
             pltpu.VMEM((STEPS // 2, blocks, LANES), jnp.float32),

time: 28.7 us -> 28.7 us (level)
  no operation moved by 1% of the time
where the time goes in v6:
time: 28.7 us; the launch traced here: 28.5 us
  blocking collectives  24.6 us (86%)
  Pallas kernels  3.85 us (13%)
    all_to_all x1, blocking collectives, by_bins(): lax.all_to_all(summed, ('blk', 'grp'), split_axis=0, concat_axis=0, tiled...  14 us
    all_to_all x1, blocking collectives, by_bins(): got = lax.all_to_all(sent, 'blk', split_axis=0, concat_axis=0, tiled=True)  10.6 us
    pallas_call x1, Pallas kernels, pairs(): pl.pallas_call(pair_kernel, out_shape=pltpu.VMEM((blocks * groups, VS_DEV...  1.67 us
    pallas_call x1, Pallas kernels, lags_of(): pl.pallas_call(lag_kernel, out_shape=jax.ShapeDtypeStruct((VS_DEV, 2 * wa...  1.13 us
    pallas_call x1, Pallas kernels, pack(): pl.pallas_call(pack_kernel, out_shape=pltpu.VMEM((blocks, SPEC_TILES + 1,...  1.05 us

profile of v6, /device:TPU:0, one launch (start us, length us, event | category | flops | bytes accessed | tf_op | source)
XLA Modules:
  0.0 28.5 jit_solution(12229212680245353605)
XLA Ops:
  0.0 1.1 %shard_map.82 = bf16[8,17,4,128]{3,2,1,0:T(4,128)(2,1)S(1)} custom-call(bf16[16,4,1024]{2,1,0:T(4,128)(2,1)} %bitcast.6, s32[4,8]{1,0:T(4,128)} %bitcast.7, s32[2,2,6]{2,1,0:T(2,128)} %bitcast.8, s32[1,384]{1,0:T(1,128)} %bitcast.9, s32[384]{0:T(512)} %local_hbm.1), custom_call_target="tpu_custom_call" | custom-call | tf_op jit(solution)/shard_map/pallas_call | solution.py:77
  1.1 10.6 %all_to_all.10.got_ref = bf16[8,17,4,128]{3,2,1,0:T(4,128)(2,1)S(1)} all-to-all(bf16[8,17,4,128]{3,2,1,0:T(4,128)(2,1)S(1)} %shard_map.82), channel_id=1, replica_groups=mesh['blk'=8,'grp'=4] {'blk'}, dimensions={0} | all-to-all | bytes 278528 | tf_op jit(solution)/shard_map/all_to_all | solution.py:264
  11.6 1.7 %shard_map.83 = bf16[32,16,256]{2,1,0:T(8,128)(2,1)S(1)} custom-call(bf16[8,17,4,128]{3,2,1,0:T(4,128)(2,1)S(1)} %all_to_all.10.got_ref, f32[32,8,128]{2,1,0:T(8,128)} %constant.6.clone.lead_hbm), custom_call_target="tpu_custom_call" | custom-call | tf_op jit(solution)/shard_map/pallas_call | solution.py:186
  13.3 0.0 copy-start
  13.3 0.0 copy-start.1
  13.4 14.0 %all_to_all.11.bins_ref = bf16[32,16,256]{2,1,0:T(8,128)(2,1)S(1)} all-to-all(bf16[32,16,256]{2,1,0:T(8,128)(2,1)S(1)} %shard_map.83), channel_id=1, replica_groups=mesh['blk'=8,'grp'=4] {'blk','grp'}, dimensions={0} | all-to-all | bytes 524288 | tf_op jit(solution)/shard_map/all_to_all | solution.py:266
  27.3 0.0 copy-done
  27.3 0.0 copy-done.1
  27.3 1.1 %shard_map.84 = f32[16,512]{1,0:T(8,128)} custom-call(bf16[32,16,256]{2,1,0:T(8,128)(2,1)S(1)} %all_to_all.11.bins_ref, bf16[2,256,256]{2,1,0:T(8,128)(2,1)S(1)} %copy-done, f32[2,32,128]{2,1,0:T(8,128)S(1)} %copy-done.1), custom_call_target="tpu_custom_call" | custom-call | tf_op jit(solution)/shard_map/pallas_call | solution.py:227
Async XLA Ops:
  13.3 14.0 %copy-start = (bf16[2,256,256]{2,1,0:T(8,128)(2,1)S(1)}, bf16[2,256,256]{2,1,0:T(8,128)(2,1)}, u32[]{:S(2)}) copy-start(bf16[2,256,256]{2,1,0:T(8,128)(2,1)} %constant.7.clone.wave_ref) | copy-start | bytes 786436
  13.3 14.0 %copy-start.1 = (f32[2,32,128]{2,1,0:T(8,128)S(1)}, f32[2,32,128]{2,1,0:T(8,128)}, u32[]{:S(2)}) copy-start(f32[2,32,128]{2,1,0:T(8,128)} %constant.8.clone.turn_ref) | copy-start | bytes 98308

commit v7 on v6

--- a/solution.py
+++ b/solution.py
@@ -1,4 +1,3 @@
-import functools
 import math
 
 import jax
@@ -115,26 +114,45 @@
     lane_out = lax.broadcasted_iota(jnp.int32, (LANES, LANES), 1)
     turned = lane_out // tile_rows * tile_rows + lane_out % STA * STA + lane_out % tile_rows // STA
     swap = (lane_in == turned).astype(jnp.float32).astype(jnp.bfloat16)
-    for chunk in range(STEPS // 2):
-        here = meta[pl.ds(chunk, blocks, stride=WIN), :]
-        if chunk:
-            other = jnp.dot(here.astype(jnp.bfloat16), swap, preferred_element_type=jnp.float32)
-            if chunk == 1:
-                block_of = lax.broadcasted_iota(jnp.int32, here.shape, 0)
-                lane = lax.broadcasted_iota(jnp.int32, here.shape, 1)
-                other = jnp.where((block_of >= blocks // 2) & (lane >= tile_rows), other, here)
-            here = other
-        names[chunk] = here
+    labels = [meta[pl.ds(chunk, blocks, stride=WIN), :] for chunk in range(STEPS // 2)]
+    turned_labels = [
+        jnp.dot(each.astype(jnp.bfloat16), swap, preferred_element_type=jnp.float32) for each in labels[1:]
+    ]
+    names[0], names[1] = labels[0], labels[1]
+    names[2], names[3] = turned_labels[1], turned_labels[0]
+    names[4], names[5] = pltpu.roll(labels[1], tile_rows, 1), pltpu.roll(turned_labels[1], tile_rows, 1)
+
+    def name(kind, block):
+        return names[kind, block % blocks : block % blocks + 1, :]
+
     source = lax.broadcasted_iota(jnp.int32, (sources, LANES), 0).astype(jnp.float32).astype(jnp.bfloat16)
     one, zero = jnp.ones((HALF_TILE, LANES), jnp.bfloat16), jnp.zeros((HALF_TILE, LANES), jnp.bfloat16)
-    for block in range(blocks):
-        for chunk in range(STEPS // 2):
-            at = (block * STEPS + 2 * chunk) * tile_rows
-            label = names[chunk, block : block + 1, :]
-            wanted = jnp.broadcast_to(label, (HALF_TILE, LANES)).astype(jnp.bfloat16)
-            for first in range(0, sources, HALF_TILE):
-                rows = slice(first, first + HALF_TILE)
-                hot[rows, at : at + LANES] = jnp.where(source[rows] == wanted, one, zero)
+    low = lax.broadcasted_iota(jnp.int32, (1, LANES), 1) < tile_rows
+    half = blocks // 2
+    pairs_of = [(name(0, block), jnp.where(low, -1.0, name(2, block - 2))) for block in range(blocks)]
+    pairs_of += [(name(1, block), jnp.where(low, name(2, block - 3), name(3, block + half))) for block in range(half)]
+    pairs_of += [
+        (
+            jnp.where(low, name(1, block), name(4, block + 1)),
+            jnp.where(low, name(2, block - 3), name(5, block - 2)),
+        )
+        for block in range(half, blocks, 2)
+    ]
+    for chunk, both in enumerate(pairs_of):
+        at = slice(chunk * LANES, (chunk + 1) * LANES)
+        forth, back = [jnp.broadcast_to(each, (HALF_TILE, LANES)).astype(jnp.bfloat16) for each in both]
+        for first in range(0, sources, HALF_TILE):
+            here = source[first : first + HALF_TILE]
+            own_rows, far_rows = jnp.where(here == forth, one, zero), jnp.where(here == back, one, zero)
+            hot[first : first + HALF_TILE, at] = own_rows + far_rows
+            hot[sources + first : sources + first + HALF_TILE, at] = own_rows - far_rows
+
+    def row_of(block, step):
+        if step < 2:
+            return block * LANES + step * tile_rows
+        if block < half:
+            return (blocks + block) * LANES + (step - 2) * tile_rows
+        return (blocks + half) * LANES + (block - half) * tile_rows
 
     for block in range(blocks):
         steps = STEPS // 2 + (block < blocks // 2)
@@ -160,19 +178,14 @@
                     rows.append((real * factor, imag * factor))
                 real = jnp.concatenate([rows[0][0], rows[1][0]], axis=0).astype(jnp.bfloat16)
                 imag = jnp.concatenate([rows[0][1], rows[1][1]], axis=0).astype(jnp.bfloat16)
-                at = (block * STEPS + step) * tile_rows + near * STA
+                at = row_of(block, step) + near * STA
                 phat[at : at + 2 * STA, :LANES] = real
                 phat[at : at + 2 * STA, LANES:] = imag
-                back = blocks - 2 - step
-                if back < STEPS:
-                    at = (far_block * STEPS + back) * tile_rows + near * STA
-                    phat[at : at + 2 * STA, :LANES] = real
-                    phat[at : at + 2 * STA, LANES:] = -imag
     total[...] = jnp.dot(hot[...], phat[...], preferred_element_type=jnp.float32)
     lead_move.wait()
     for block in range(blocks):
         at = slice(block * VS_DEV, (block + 1) * VS_DEV)
-        real, imag = total[at, :LANES], total[at, LANES:]
+        real, imag = total[at, :LANES], total[sources + block * VS_DEV : sources + (block + 1) * VS_DEV, LANES:]
         for group in range(groups):
             cosine, sine = lead_ref[group : group + 1, :], lead_ref[groups + group : groups + group + 1, :]
             out_ref[block * groups + group] = jnp.concatenate(
@@ -182,7 +195,7 @@
 
 def pairs(got, lead):
     blocks, groups = got.shape[0], lead.shape[1] // 2
-    sources, rows = blocks * VS_DEV, blocks * STEPS * STA * STA
+    sources, rows = blocks * VS_DEV, blocks * STEPS * STA * STA * 7 // 12
     return pl.pallas_call(
         pair_kernel,
         out_shape=pltpu.VMEM((blocks * groups, VS_DEV, 2 * LANES), jnp.bfloat16),
@@ -195,10 +208,10 @@
             pltpu.VMEM((blocks * WIN + STA, LANES), jnp.float32),
             pltpu.VMEM((blocks, 3 * WIN, STA, LANES), jnp.float32),
             pltpu.VMEM((blocks, 3 * WIN, STA, LANES), jnp.float32),
-            pltpu.VMEM((STEPS // 2, blocks, LANES), jnp.float32),
+            pltpu.VMEM((STEPS, blocks, LANES), jnp.float32),
             pltpu.VMEM((rows, 2 * LANES), jnp.bfloat16),
-            pltpu.VMEM((sources, rows), jnp.bfloat16),
-            pltpu.VMEM((sources, 2 * LANES), jnp.float32),
+            pltpu.VMEM((2 * sources, rows), jnp.bfloat16),
+            pltpu.VMEM((2 * sources, 2 * LANES), jnp.float32),
             pltpu.SemaphoreType.DMA,
         ],
     )(got, pltpu.with_memory_space_constraint(lead, pltpu.HBM))

time: 28.7 us -> 28.6 us (level)
  no operation moved by 1% of the time
where the time goes in v7:
time: 28.6 us; the launch traced here: 28.4 us
  blocking collectives  24.6 us (86%)
  Pallas kernels  3.78 us (13%)
    all_to_all x1, blocking collectives, by_bins(): lax.all_to_all(summed, ('blk', 'grp'), split_axis=0, concat_axis=0, tiled...  14 us
    all_to_all x1, blocking collectives, by_bins(): got = lax.all_to_all(sent, 'blk', split_axis=0, concat_axis=0, tiled=True)  10.6 us
    pallas_call x1, Pallas kernels, pairs(): pl.pallas_call(pair_kernel, out_shape=pltpu.VMEM((blocks * groups, VS_DEV...  1.6 us
    pallas_call x1, Pallas kernels, lags_of(): pl.pallas_call(lag_kernel, out_shape=jax.ShapeDtypeStruct((VS_DEV, 2 * wa...  1.13 us
    pallas_call x1, Pallas kernels, pack(): pl.pallas_call(pack_kernel, out_shape=pltpu.VMEM((blocks, SPEC_TILES + 1,...  1.05 us

profile of v7, /device:TPU:0, one launch (start us, length us, event | category | flops | bytes accessed | tf_op | source)
XLA Modules:
  0.0 28.4 jit_solution(9614386178473594675)
XLA Ops:
  0.0 1.1 %shard_map.82 = bf16[8,17,4,128]{3,2,1,0:T(4,128)(2,1)S(1)} custom-call(bf16[16,4,1024]{2,1,0:T(4,128)(2,1)} %bitcast.6, s32[4,8]{1,0:T(4,128)} %bitcast.7, s32[2,2,6]{2,1,0:T(2,128)} %bitcast.8, s32[1,384]{1,0:T(1,128)} %bitcast.9, s32[384]{0:T(512)} %local_hbm.1), custom_call_target="tpu_custom_call" | custom-call | tf_op jit(solution)/shard_map/pallas_call | solution.py:76
  1.1 10.6 %all_to_all.10.got_ref = bf16[8,17,4,128]{3,2,1,0:T(4,128)(2,1)S(1)} all-to-all(bf16[8,17,4,128]{3,2,1,0:T(4,128)(2,1)S(1)} %shard_map.82), channel_id=1, replica_groups=mesh['blk'=8,'grp'=4] {'blk'}, dimensions={0} | all-to-all | bytes 278528 | tf_op jit(solution)/shard_map/all_to_all | solution.py:277
  11.6 1.6 %shard_map.83 = bf16[32,16,256]{2,1,0:T(8,128)(2,1)S(1)} custom-call(bf16[8,17,4,128]{3,2,1,0:T(4,128)(2,1)S(1)} %all_to_all.10.got_ref, f32[32,8,128]{2,1,0:T(8,128)} %constant.6.clone.lead_hbm), custom_call_target="tpu_custom_call" | custom-call | tf_op jit(solution)/shard_map/pallas_call | solution.py:199
  13.3 0.0 copy-start
  13.3 0.0 copy-start.1
  13.3 14.0 %all_to_all.11.bins_ref = bf16[32,16,256]{2,1,0:T(8,128)(2,1)S(1)} all-to-all(bf16[32,16,256]{2,1,0:T(8,128)(2,1)S(1)} %shard_map.83), channel_id=1, replica_groups=mesh['blk'=8,'grp'=4] {'blk','grp'}, dimensions={0} | all-to-all | bytes 524288 | tf_op jit(solution)/shard_map/all_to_all | solution.py:279
  27.3 0.0 copy-done
  27.3 0.0 copy-done.1
  27.3 1.1 %shard_map.84 = f32[16,512]{1,0:T(8,128)} custom-call(bf16[32,16,256]{2,1,0:T(8,128)(2,1)S(1)} %all_to_all.11.bins_ref, bf16[2,256,256]{2,1,0:T(8,128)(2,1)S(1)} %copy-done, f32[2,32,128]{2,1,0:T(8,128)S(1)} %copy-done.1), custom_call_target="tpu_custom_call" | custom-call | tf_op jit(solution)/shard_map/pallas_call | solution.py:240
Async XLA Ops:
  13.3 14.0 %copy-start = (bf16[2,256,256]{2,1,0:T(8,128)(2,1)S(1)}, bf16[2,256,256]{2,1,0:T(8,128)(2,1)}, u32[]{:S(2)}) copy-start(bf16[2,256,256]{2,1,0:T(8,128)(2,1)} %constant.7.clone.wave_ref) | copy-start | bytes 786436
  13.3 14.0 %copy-start.1 = (f32[2,32,128]{2,1,0:T(8,128)S(1)}, f32[2,32,128]{2,1,0:T(8,128)}, u32[]{:S(2)}) copy-start(f32[2,32,128]{2,1,0:T(8,128)} %constant.8.clone.turn_ref) | copy-start | bytes 98308

commit v8 on v7

--- a/solution.py
+++ b/solution.py
@@ -183,12 +183,13 @@
                 phat[at : at + 2 * STA, LANES:] = imag
     total[...] = jnp.dot(hot[...], phat[...], preferred_element_type=jnp.float32)
     lead_move.wait()
+    order = peer_order(blocks, groups)
     for block in range(blocks):
         at = slice(block * VS_DEV, (block + 1) * VS_DEV)
         real, imag = total[at, :LANES], total[sources + block * VS_DEV : sources + (block + 1) * VS_DEV, LANES:]
         for group in range(groups):
             cosine, sine = lead_ref[group : group + 1, :], lead_ref[groups + group : groups + group + 1, :]
-            out_ref[block * groups + group] = jnp.concatenate(
+            out_ref[order.index(block * groups + group)] = jnp.concatenate(
                 [real * cosine - imag * sine, real * sine + imag * cosine], axis=1
             ).astype(jnp.bfloat16)
 
@@ -264,10 +265,15 @@
     wave = np.stack(tiles) / math.sqrt(BINS)
     high = wave.astype(jnp.bfloat16)
     low = (wave - high.astype(np.float64)).astype(jnp.bfloat16)
-    place = np.arange(chunks)
+    place = np.array(peer_order(blocks, groups))
     chunk = place % groups * blocks + place // groups
     turn = np.stack(turns(LANES * chunk[:, None] * (bins + 0.5))).astype(np.float32)
     return jnp.asarray(lead), jnp.asarray(np.concatenate([high, low], axis=1)), jnp.asarray(turn)
+
+
+def peer_order(blocks, groups):
+    first = [0, groups]
+    return first + [device for device in range(blocks * groups) if device not in first]
 
 
 def by_bins(spectra, quality, pair_mask, owners, local_rows):
@@ -276,7 +282,10 @@
     sent = pack(spectra, quality, pair_mask, owners, local_rows, blocks)
     got = lax.all_to_all(sent, "blk", split_axis=0, concat_axis=0, tiled=True)
     summed = pairs(got, lead)
-    bins = lax.all_to_all(summed, ("blk", "grp"), split_axis=0, concat_axis=0, tiled=True)
+    order = [peer_order(blocks, groups)]
+    bins = lax.all_to_all(
+        summed, ("blk", "grp"), split_axis=0, concat_axis=0, tiled=True, axis_index_groups=order
+    )
     return lags_of(bins, wave, turn)
 
 

time: 28.6 us -> 28.5 us (level)
  no operation moved by 1% of the time
where the time goes in v8:
time: 28.5 us; the launch traced here: 28.2 us
  blocking collectives  24.4 us (86%)
  Pallas kernels  3.78 us (13%)
    all_to_all x1, blocking collectives, by_bins(): lax.all_to_all(summed, ('blk', 'grp'), split_axis=0, concat_axis=0, tiled...  13.8 us
    all_to_all x1, blocking collectives, by_bins(): got = lax.all_to_all(sent, 'blk', split_axis=0, concat_axis=0, tiled=True)  10.6 us
    pallas_call x1, Pallas kernels, pairs(): pl.pallas_call(pair_kernel, out_shape=pltpu.VMEM((blocks * groups, VS_DEV...  1.6 us
    pallas_call x1, Pallas kernels, lags_of(): pl.pallas_call(lag_kernel, out_shape=jax.ShapeDtypeStruct((VS_DEV, 2 * wa...  1.13 us
    pallas_call x1, Pallas kernels, pack(): pl.pallas_call(pack_kernel, out_shape=pltpu.VMEM((blocks, SPEC_TILES + 1,...  1.05 us

profile of v8, /device:TPU:0, one launch (start us, length us, event | category | flops | bytes accessed | tf_op | source)
XLA Modules:
  0.0 28.2 jit_solution(5863775484540464357)
XLA Ops:
  0.0 1.1 %shard_map.82 = bf16[8,17,4,128]{3,2,1,0:T(4,128)(2,1)S(1)} custom-call(bf16[16,4,1024]{2,1,0:T(4,128)(2,1)} %bitcast.6, s32[4,8]{1,0:T(4,128)} %bitcast.7, s32[2,2,6]{2,1,0:T(2,128)} %bitcast.8, s32[1,384]{1,0:T(1,128)} %bitcast.9, s32[384]{0:T(512)} %local_hbm.1), custom_call_target="tpu_custom_call" | custom-call | tf_op jit(solution)/shard_map/pallas_call | solution.py:76
  1.1 10.6 %all_to_all.10.got_ref = bf16[8,17,4,128]{3,2,1,0:T(4,128)(2,1)S(1)} all-to-all(bf16[8,17,4,128]{3,2,1,0:T(4,128)(2,1)S(1)} %shard_map.82), channel_id=1, replica_groups=mesh['blk'=8,'grp'=4] {'blk'}, dimensions={0} | all-to-all | bytes 278528 | tf_op jit(solution)/shard_map/all_to_all | solution.py:283
  11.6 1.6 %shard_map.83 = bf16[32,16,256]{2,1,0:T(8,128)(2,1)S(1)} custom-call(bf16[8,17,4,128]{3,2,1,0:T(4,128)(2,1)S(1)} %all_to_all.10.got_ref, f32[32,8,128]{2,1,0:T(8,128)} %constant.6.clone.lead_hbm), custom_call_target="tpu_custom_call" | custom-call | tf_op jit(solution)/shard_map/pallas_call | solution.py:200
  13.3 0.0 copy-start
  13.3 0.0 copy-start.1
  13.3 13.8 %all_to_all.11.bins_ref = bf16[32,16,256]{2,1,0:T(8,128)(2,1)S(1)} all-to-all(bf16[32,16,256]{2,1,0:T(8,128)(2,1)S(1)} %shard_map.83), channel_id=1, replica_groups={{0,4,1,2,3,5,6,7,8,9,10,11,12,13,14,15,16,17,18,19,20,21,22,23,24,25,26..., dimensions={0} | all-to-all | bytes 524288 | tf_op jit(solution)/shard_map/all_to_all | solution.py:286
  27.1 0.0 copy-done
  27.1 0.0 copy-done.1
  27.1 1.1 %shard_map.84 = f32[16,512]{1,0:T(8,128)} custom-call(bf16[32,16,256]{2,1,0:T(8,128)(2,1)S(1)} %all_to_all.11.bins_ref, bf16[2,256,256]{2,1,0:T(8,128)(2,1)S(1)} %copy-done, f32[2,32,128]{2,1,0:T(8,128)S(1)} %copy-done.1), custom_call_target="tpu_custom_call" | custom-call | tf_op jit(solution)/shard_map/pallas_call | solution.py:241
Async XLA Ops:
  13.3 13.8 %copy-start = (bf16[2,256,256]{2,1,0:T(8,128)(2,1)S(1)}, bf16[2,256,256]{2,1,0:T(8,128)(2,1)}, u32[]{:S(2)}) copy-start(bf16[2,256,256]{2,1,0:T(8,128)(2,1)} %constant.7.clone.wave_ref) | copy-start | bytes 786436
  13.3 13.8 %copy-start.1 = (f32[2,32,128]{2,1,0:T(8,128)S(1)}, f32[2,32,128]{2,1,0:T(8,128)}, u32[]{:S(2)}) copy-start(f32[2,32,128]{2,1,0:T(8,128)} %constant.8.clone.turn_ref) | copy-start | bytes 98308

commit v9 on v7

--- a/solution.py
+++ b/solution.py
@@ -106,7 +106,7 @@
             column = jnp.sum(mine, axis=1, keepdims=True)
             real = plain[block, pl.ds(window, STA, stride=WIN), :] * column
             imag = plain[block, pl.ds(STA * WIN + window, STA, stride=WIN), :] * column
-            for place, (near, far) in enumerate([(real, real), (imag, imag), (real + imag, real - imag)]):
+            for place, (near, far) in enumerate([(real + imag, real), (real, real + imag), (imag, real - imag)]):
                 own_spec[block, place * WIN + window] = near
                 far_spec[block, place * WIN + window] = far
 
@@ -173,7 +173,7 @@
                         sum(own[more][place] * far[place] for place in range(kind * WIN, (kind + 1) * WIN))
                         for kind in range(3)
                     ]
-                    real, imag = sums[0] + sums[1], sums[2] - sums[0] + sums[1]
+                    real, imag = sums[0] - sums[2], sums[0] - sums[1]
                     factor = lax.rsqrt(jnp.maximum(real * real + imag * imag, 1.0))
                     rows.append((real * factor, imag * factor))
                 real = jnp.concatenate([rows[0][0], rows[1][0]], axis=0).astype(jnp.bfloat16)

time: 28.6 us -> 28.6 us (level)
  no operation moved by 1% of the time
where the time goes in v9:
time: 28.6 us; the launch traced here: 28.4 us
  blocking collectives  24.6 us (86%)
  Pallas kernels  3.75 us (13%)
    all_to_all x1, blocking collectives, by_bins(): lax.all_to_all(summed, ('blk', 'grp'), split_axis=0, concat_axis=0, tiled...  14 us
    all_to_all x1, blocking collectives, by_bins(): got = lax.all_to_all(sent, 'blk', split_axis=0, concat_axis=0, tiled=True)  10.6 us
    pallas_call x1, Pallas kernels, pairs(): pl.pallas_call(pair_kernel, out_shape=pltpu.VMEM((blocks * groups, VS_DEV...  1.57 us
    pallas_call x1, Pallas kernels, lags_of(): pl.pallas_call(lag_kernel, out_shape=jax.ShapeDtypeStruct((VS_DEV, 2 * wa...  1.13 us
    pallas_call x1, Pallas kernels, pack(): pl.pallas_call(pack_kernel, out_shape=pltpu.VMEM((blocks, SPEC_TILES + 1,...  1.05 us

profile of v9, /device:TPU:0, one launch (start us, length us, event | category | flops | bytes accessed | tf_op | source)
XLA Modules:
  0.0 28.4 jit_solution(17189447365411540373)
XLA Ops:
  0.0 1.1 %shard_map.82 = bf16[8,17,4,128]{3,2,1,0:T(4,128)(2,1)S(1)} custom-call(bf16[16,4,1024]{2,1,0:T(4,128)(2,1)} %bitcast.6, s32[4,8]{1,0:T(4,128)} %bitcast.7, s32[2,2,6]{2,1,0:T(2,128)} %bitcast.8, s32[1,384]{1,0:T(1,128)} %bitcast.9, s32[384]{0:T(512)} %local_hbm.1), custom_call_target="tpu_custom_call" | custom-call | tf_op jit(solution)/shard_map/pallas_call | solution.py:76
  1.1 10.6 %all_to_all.10.got_ref = bf16[8,17,4,128]{3,2,1,0:T(4,128)(2,1)S(1)} all-to-all(bf16[8,17,4,128]{3,2,1,0:T(4,128)(2,1)S(1)} %shard_map.82), channel_id=1, replica_groups=mesh['blk'=8,'grp'=4] {'blk'}, dimensions={0} | all-to-all | bytes 278528 | tf_op jit(solution)/shard_map/all_to_all | solution.py:277
  11.6 1.6 %shard_map.83 = bf16[32,16,256]{2,1,0:T(8,128)(2,1)S(1)} custom-call(bf16[8,17,4,128]{3,2,1,0:T(4,128)(2,1)S(1)} %all_to_all.10.got_ref, f32[32,8,128]{2,1,0:T(8,128)} %constant.6.clone.lead_hbm), custom_call_target="tpu_custom_call" | custom-call | tf_op jit(solution)/shard_map/pallas_call | solution.py:199
  13.2 0.0 copy-start
  13.2 0.0 copy-start.1
  13.2 14.0 %all_to_all.11.bins_ref = bf16[32,16,256]{2,1,0:T(8,128)(2,1)S(1)} all-to-all(bf16[32,16,256]{2,1,0:T(8,128)(2,1)S(1)} %shard_map.83), channel_id=1, replica_groups=mesh['blk'=8,'grp'=4] {'blk','grp'}, dimensions={0} | all-to-all | bytes 524288 | tf_op jit(solution)/shard_map/all_to_all | solution.py:279
  27.2 0.0 copy-done
  27.2 0.0 copy-done.1
  27.2 1.1 %shard_map.84 = f32[16,512]{1,0:T(8,128)} custom-call(bf16[32,16,256]{2,1,0:T(8,128)(2,1)S(1)} %all_to_all.11.bins_ref, bf16[2,256,256]{2,1,0:T(8,128)(2,1)S(1)} %copy-done, f32[2,32,128]{2,1,0:T(8,128)S(1)} %copy-done.1), custom_call_target="tpu_custom_call" | custom-call | tf_op jit(solution)/shard_map/pallas_call | solution.py:240
Async XLA Ops:
  13.2 14.0 %copy-start = (bf16[2,256,256]{2,1,0:T(8,128)(2,1)S(1)}, bf16[2,256,256]{2,1,0:T(8,128)(2,1)}, u32[]{:S(2)}) copy-start(bf16[2,256,256]{2,1,0:T(8,128)(2,1)} %constant.7.clone.wave_ref) | copy-start | bytes 786436
  13.2 14.0 %copy-start.1 = (f32[2,32,128]{2,1,0:T(8,128)S(1)}, f32[2,32,128]{2,1,0:T(8,128)}, u32[]{:S(2)}) copy-start(f32[2,32,128]{2,1,0:T(8,128)} %constant.8.clone.turn_ref) | copy-start | bytes 98308

commit v10 on v7

--- a/solution.py
+++ b/solution.py
@@ -129,8 +129,11 @@
     one, zero = jnp.ones((HALF_TILE, LANES), jnp.bfloat16), jnp.zeros((HALF_TILE, LANES), jnp.bfloat16)
     low = lax.broadcasted_iota(jnp.int32, (1, LANES), 1) < tile_rows
     half = blocks // 2
-    pairs_of = [(name(0, block), jnp.where(low, -1.0, name(2, block - 2))) for block in range(blocks)]
-    pairs_of += [(name(1, block), jnp.where(low, name(2, block - 3), name(3, block + half))) for block in range(half)]
+    pairs_of = []
+    for block in range(blocks):
+        pairs_of.append((name(0, block), jnp.where(low, -1.0, name(2, block - 2))))
+        if block < half:
+            pairs_of.append((name(1, block), jnp.where(low, name(2, block - 3), name(3, block + half))))
     pairs_of += [
         (
             jnp.where(low, name(1, block), name(4, block + 1)),
@@ -148,10 +151,10 @@
             hot[sources + first : sources + first + HALF_TILE, at] = own_rows - far_rows
 
     def row_of(block, step):
+        if block < half:
+            return 2 * block * LANES + step * tile_rows
         if step < 2:
-            return block * LANES + step * tile_rows
-        if block < half:
-            return (blocks + block) * LANES + (step - 2) * tile_rows
+            return (block + half) * LANES + step * tile_rows
         return (blocks + half) * LANES + (block - half) * tile_rows
 
     for block in range(blocks):
@@ -181,11 +184,17 @@
                 at = row_of(block, step) + near * STA
                 phat[at : at + 2 * STA, :LANES] = real
                 phat[at : at + 2 * STA, LANES:] = imag
-    total[...] = jnp.dot(hot[...], phat[...], preferred_element_type=jnp.float32)
+        if block == half:
+            both = jnp.dot(hot[:, :1024], phat[:1024, :], preferred_element_type=jnp.float32)
+            total[0] = both[:sources, :LANES]
+            total[1] = both[sources:, LANES:]
+    both = jnp.dot(hot[:, 1024:], phat[1024:, :], preferred_element_type=jnp.float32)
+    total[0] += both[:sources, :LANES]
+    total[1] += both[sources:, LANES:]
     lead_move.wait()
     for block in range(blocks):
         at = slice(block * VS_DEV, (block + 1) * VS_DEV)
-        real, imag = total[at, :LANES], total[sources + block * VS_DEV : sources + (block + 1) * VS_DEV, LANES:]
+        real, imag = total[0, at, :], total[1, at, :]
         for group in range(groups):
             cosine, sine = lead_ref[group : group + 1, :], lead_ref[groups + group : groups + group + 1, :]
             out_ref[block * groups + group] = jnp.concatenate(
@@ -211,7 +220,7 @@
             pltpu.VMEM((STEPS, blocks, LANES), jnp.float32),
             pltpu.VMEM((rows, 2 * LANES), jnp.bfloat16),
             pltpu.VMEM((2 * sources, rows), jnp.bfloat16),
-            pltpu.VMEM((2 * sources, 2 * LANES), jnp.float32),
+            pltpu.VMEM((2, sources, LANES), jnp.float32),
             pltpu.SemaphoreType.DMA,
         ],
     )(got, pltpu.with_memory_space_constraint(lead, pltpu.HBM))

time: 28.6 us -> 28.6 us (level)
  no operation moved by 1% of the time
where the time goes in v10:
time: 28.6 us; the launch traced here: 28.4 us
  blocking collectives  24.6 us (86%)
  Pallas kernels  3.78 us (13%)
    all_to_all x1, blocking collectives, by_bins(): lax.all_to_all(summed, ('blk', 'grp'), split_axis=0, concat_axis=0, tiled...  14 us
    all_to_all x1, blocking collectives, by_bins(): got = lax.all_to_all(sent, 'blk', split_axis=0, concat_axis=0, tiled=True)  10.6 us
    pallas_call x1, Pallas kernels, pairs(): pl.pallas_call(pair_kernel, out_shape=pltpu.VMEM((blocks * groups, VS_DEV...  1.6 us
    pallas_call x1, Pallas kernels, lags_of(): pl.pallas_call(lag_kernel, out_shape=jax.ShapeDtypeStruct((VS_DEV, 2 * wa...  1.13 us
    pallas_call x1, Pallas kernels, pack(): pl.pallas_call(pack_kernel, out_shape=pltpu.VMEM((blocks, SPEC_TILES + 1,...  1.05 us

profile of v10, /device:TPU:0, one launch (start us, length us, event | category | flops | bytes accessed | tf_op | source)
XLA Modules:
  0.0 28.4 jit_solution(14660317357177022093)
XLA Ops:
  0.0 1.1 %shard_map.82 = bf16[8,17,4,128]{3,2,1,0:T(4,128)(2,1)S(1)} custom-call(bf16[16,4,1024]{2,1,0:T(4,128)(2,1)} %bitcast.6, s32[4,8]{1,0:T(4,128)} %bitcast.7, s32[2,2,6]{2,1,0:T(2,128)} %bitcast.8, s32[1,384]{1,0:T(1,128)} %bitcast.9, s32[384]{0:T(512)} %local_hbm.1), custom_call_target="tpu_custom_call" | custom-call | tf_op jit(solution)/shard_map/pallas_call | solution.py:76
  1.1 10.6 %all_to_all.10.got_ref = bf16[8,17,4,128]{3,2,1,0:T(4,128)(2,1)S(1)} all-to-all(bf16[8,17,4,128]{3,2,1,0:T(4,128)(2,1)S(1)} %shard_map.82), channel_id=1, replica_groups=mesh['blk'=8,'grp'=4] {'blk'}, dimensions={0} | all-to-all | bytes 278528 | tf_op jit(solution)/shard_map/all_to_all | solution.py:286
  11.6 1.6 %shard_map.83 = bf16[32,16,256]{2,1,0:T(8,128)(2,1)S(1)} custom-call(bf16[8,17,4,128]{3,2,1,0:T(4,128)(2,1)S(1)} %all_to_all.10.got_ref, f32[32,8,128]{2,1,0:T(8,128)} %constant.6.clone.lead_hbm), custom_call_target="tpu_custom_call" | custom-call | tf_op jit(solution)/shard_map/pallas_call | solution.py:208
  13.3 0.0 copy-start
  13.3 0.0 copy-start.1
  13.3 14.0 %all_to_all.11.bins_ref = bf16[32,16,256]{2,1,0:T(8,128)(2,1)S(1)} all-to-all(bf16[32,16,256]{2,1,0:T(8,128)(2,1)S(1)} %shard_map.83), channel_id=1, replica_groups=mesh['blk'=8,'grp'=4] {'blk','grp'}, dimensions={0} | all-to-all | bytes 524288 | tf_op jit(solution)/shard_map/all_to_all | solution.py:288
  27.3 0.0 copy-done
  27.3 0.0 copy-done.1
  27.3 1.1 %shard_map.84 = f32[16,512]{1,0:T(8,128)} custom-call(bf16[32,16,256]{2,1,0:T(8,128)(2,1)S(1)} %all_to_all.11.bins_ref, bf16[2,256,256]{2,1,0:T(8,128)(2,1)S(1)} %copy-done, f32[2,32,128]{2,1,0:T(8,128)S(1)} %copy-done.1), custom_call_target="tpu_custom_call" | custom-call | tf_op jit(solution)/shard_map/pallas_call | solution.py:249
Async XLA Ops:
  13.3 14.0 %copy-start = (bf16[2,256,256]{2,1,0:T(8,128)(2,1)S(1)}, bf16[2,256,256]{2,1,0:T(8,128)(2,1)}, u32[]{:S(2)}) copy-start(bf16[2,256,256]{2,1,0:T(8,128)(2,1)} %constant.7.clone.wave_ref) | copy-start | bytes 786436
  13.3 14.0 %copy-start.1 = (f32[2,32,128]{2,1,0:T(8,128)S(1)}, f32[2,32,128]{2,1,0:T(8,128)}, u32[]{:S(2)}) copy-start(f32[2,32,128]{2,1,0:T(8,128)} %constant.8.clone.turn_ref) | copy-start | bytes 98308
